TPU v7x, 32 devices: a whole 2x2x4 slice. The times are simulated.
32 devices in a mesh: tm: 8 (over y, x, core), space: 4 (over z).
Axes of the slice: x: 2, y: 2, z: 4, core: 2. Of those that a mesh axis runs over, the one named last changes fastest.
Arguments:
- video: bfloat16 [32, 1152, 1536], P('tm', 'space'), may hold values from -6 to 6
- frame_count: int32 [1], replicated, may hold values from 8 to 32
- qkv_space: bfloat16 [1536, 3072], replicated, may hold values from -0.15625 to 0.15625
- out_space: bfloat16 [1024, 1536], replicated, may hold values from -0.1875 to 0.1875
- qkv_time: bfloat16 [1536, 3072], replicated, may hold values from -0.15625 to 0.15625
- out_time: bfloat16 [1024, 1536], replicated, may hold values from -0.1875 to 0.1875
Outputs:
- encoded: bfloat16 [32, 1152, 1536], P('tm', 'space')
All inputs are finite; a program needn't handle non-finite values.
Results may differ from a plain program's by a relative error of at most 0.0085.
Values may be sent and summed in bfloat16 or wider, within the bound.
A program may use at most 192 MiB of HBM per device.

v0:
```python
import jax
import jax.numpy as jnp
from jax import lax
from jax.sharding import PartitionSpec as P

H = 16
HD = 64


def layer_norm(values):
    wide = values.astype(jnp.float32)
    center = wide - jnp.mean(wide, axis=-1, keepdims=True)
    spread = jnp.mean(center * center, axis=-1, keepdims=True)
    return (center * lax.rsqrt(spread + 1e-06)).astype(jnp.bfloat16)


def spatial_attend(items):
    count = items.shape[0]
    total = items.shape[1]
    local_heads = items.shape[3] // HD
    parts = items.reshape(count, total, 3, local_heads, HD)
    scores = (
        jnp.einsum(
            "fqhd,fkhd->fhqk", parts[:, :, 0], parts[:, :, 1], preferred_element_type=jnp.float32
        )
        * 0.125
    )
    weights = jax.nn.softmax(scores, axis=-1).astype(jnp.bfloat16)
    result = jnp.einsum(
        "fhqk,fkhd->fqhd", weights, parts[:, :, 2], preferred_element_type=jnp.float32
    )
    result = result.astype(jnp.bfloat16).reshape(count, total, local_heads * HD)
    return lax.all_to_all(result, "space", split_axis=1, concat_axis=2, tiled=True)


def per_device(video, frame_count, qkv_space, out_space, qkv_time, out_time):
    frames, patches, width = video.shape
    first = lax.axis_index("tm") * frames
    limit = frame_count[0]
    valid = (first + jnp.arange(frames) < limit).astype(jnp.float32)[:, None, None]
    norm1 = layer_norm(video)
    qkv1 = jnp.dot(
        norm1.reshape(frames * patches, width), qkv_space, preferred_element_type=jnp.float32
    )
    qkv1 = qkv1.astype(jnp.bfloat16).reshape(frames, patches, 3, H * HD)
    spatial = spatial_attend(lax.all_to_all(qkv1, "space", split_axis=3, concat_axis=1, tiled=True))
    branch = jnp.dot(
        spatial.reshape(frames * patches, H * HD), out_space, preferred_element_type=jnp.float32
    )
    middle = (video.astype(jnp.float32) + valid * branch.reshape(frames, patches, width)).astype(
        jnp.bfloat16
    )
    norm2 = layer_norm(middle)
    qkv2 = jnp.dot(
        norm2.reshape(frames * patches, width), qkv_time, preferred_element_type=jnp.float32
    )
    qkv2 = qkv2.astype(jnp.bfloat16).reshape(frames, patches, 3 * H * HD)
    gathered = lax.all_to_all(qkv2, "tm", split_axis=1, concat_axis=0, tiled=True)
    all_frames, few_patches = (gathered.shape[0], gathered.shape[1])
    parts = gathered.reshape(all_frames, few_patches, 3, H, HD)
    scores = (
        jnp.einsum(
            "fphd,gphd->phfg", parts[:, :, 0], parts[:, :, 1], preferred_element_type=jnp.float32
        )
        * 0.125
    )
    key_valid = jnp.arange(all_frames) < limit
    scores = jnp.where(key_valid[None, None, None, :], scores, -1e30)
    weights = jax.nn.softmax(scores, axis=-1).astype(jnp.bfloat16)
    temporal = jnp.einsum(
        "phfg,gphd->fphd", weights, parts[:, :, 2], preferred_element_type=jnp.float32
    )
    temporal = temporal.astype(jnp.bfloat16).reshape(all_frames, few_patches, H * HD)
    returned = lax.all_to_all(temporal, "tm", split_axis=0, concat_axis=1, tiled=True)
    branch2 = jnp.dot(
        returned.reshape(frames * patches, H * HD), out_time, preferred_element_type=jnp.float32
    )
    return (middle.astype(jnp.float32) + valid * branch2.reshape(frames, patches, width)).astype(
        jnp.bfloat16
    )


def solution(mesh):
    return jax.shard_map(
        per_device,
        mesh=mesh,
        in_specs=(P("tm", "space", None), P(), P(), P(), P(), P()),
        out_specs=P("tm", "space", None),
        check_vma=False,
    )
```

profile of v0, /device:TPU:29, one launch (start us, length us, event | category | flops | bytes accessed | tf_op | source)
XLA Modules:
  0.0 656.4 jit_solution(15658624417435455656)
XLA Ops:
  0.0 0.0 copy-start
  0.0 0.0 copy-start.1
  0.0 2.7 convert_reduce_fusion.1
  2.7 3.8 fusion.12
  6.6 0.0 copy-done.1
  6.6 0.9 fusion.13
  7.5 0.0 copy-done.5
  7.5 13.0 %convolution_convert_fusion.1 = bf16[1152,3072]{1,0:T(8,128)(2,1)} fusion(bf16[1152,1536]{1,0:T(8,128)(2,1)S(1)} %bitcast.87, bf16[1536,3072]{1,0:T(8,128)(2,1)S(1)} %copy-done.5), kind=kOutput, calls=%fused_computation.8 | convolution fusion | flops 10875174912 | bytes 20054016 | tf_op jit(solution)/shard_map/dot_general | solution.py:42
  20.5 19.9 %reshape.75 = bf16[4,288,3,1024]{3,2,1,0:T(4,128)(2,1)} reshape(bf16[1152,3072]{1,0:T(8,128)(2,1)} %convolution_convert_fusion.1) | data formatting | bytes 14155776 | tf_op jit(solution)/shard_map/reshape | solution.py:45
  40.4 19.6 %copy.49 = bf16[4,288,3,1024]{1,0,2,3:T(4,128)(2,1)} copy(bf16[4,288,3,1024]{3,2,1,0:T(4,128)(2,1)} %reshape.75) | data formatting | bytes 14155776 | tf_op jit(solution)/shard_map/reshape | solution.py:45
  60.0 208.6 %all_to_all.60 = bf16[4,288,3,1024]{1,0,2,3:T(4,128)(2,1)S(1)} all-to-all(bf16[4,288,3,1024]{1,0,2,3:T(4,128)(2,1)} %copy.49), channel_id=1, replica_groups=mesh['tm'=8,'space'=4] {'space'}, dimensions={3} | all-to-all | bytes 14155776 | tf_op jit(solution)/shard_map/all_to_all | solution.py:46
  268.6 7.3 %copy.77 = bf16[4,4,288,3,256]{2,1,4,0,3:T(4,128)(2,1)} copy(bf16[4,4,288,3,256]{2,0,3,4,1:T(4,128)(2,1)S(1)} %bitcast.83) | data formatting | bytes 14155776 | tf_op jit(solution)/shard_map/reshape | solution.py:21
  275.9 15.2 %reshape.85 = bf16[4,1152,3,4,64]{1,4,3,0,2:T(8,128)(2,1)} reshape(bf16[4,4,288,3,256]{2,1,4,0,3:T(4,128)(2,1)} %copy.77) | data formatting | bytes 14155776 | tf_op jit(solution)/shard_map/reshape | solution.py:21
  291.1 25.0 %fusion.34 = f32[4,4,1152]{2,1,0:T(4,128)S(1)} fusion(bf16[4,1152,3,4,64]{1,4,3,0,2:T(8,128)(2,1)} %reshape.85), kind=kOutput, calls=%fused_computation.59 | convolution fusion | flops 2781611008 | bytes 4792320 | tf_op jit(solution)/shard_map/sub | solution.py:28
  316.1 35.0 %fusion.22 = bf16[4,4,64,1152]{3,2,1,0:T(8,128)(2,1)} fusion(f32[4,4,1152]{2,1,0:T(4,128)S(1)} %fusion.34, bf16[4,1152,3,4,64]{1,4,3,0,2:T(8,128)(2,1)} %reshape.85), kind=kOutput, calls=%fused_computation.39 | convolution fusion | flops 5521951744 | bytes 9510912 | tf_op jit(solution)/shard_map/fhqk,fkhd->fqhd/dot_general | solution.py:29
  351.2 5.1 copy.56
  356.3 5.5 all-to-all-start.1
  362.5 49.4 %all-to-all-done.1 = bf16[4,1152,256]{2,0,1:T(4,128)(2,1)} async-done(((bf16[4,1152,256]{2,0,1:T(4,128)(2,1)}), bf16[4,1152,256]{2,0,1:T(4,128)(2,1)}, u32[]{:S(2)}, u32[]{:S(2)}) %all-to-all-start.1) | async-done | bytes 2359328 | tf_op jit(solution)/shard_map/all_to_all | solution.py:33
  411.9 2.1 copy.57
  414.0 0.3 copy.83
  414.3 0.0 slice-start
  414.3 0.0 copy-done
  414.3 0.2 copy-done.2
  414.6 4.4 convert_reduce_fusion
  419.0 0.0 copy-start.3
  419.0 1.1 fusion.10
  420.1 0.7 copy-done.3
  420.8 0.9 fusion.11
  421.7 0.0 slice-done
  421.7 0.0 slice-done.1
  421.7 0.0 slice-done.2
  421.7 13.2 %convolution_convert_fusion = bf16[1152,3072]{1,0:T(8,128)(2,1)} fusion(bf16[1152,1536]{1,0:T(8,128)(2,1)S(1)} %bitcast.88, bf16[1536,3072]{1,0:T(8,128)(2,1)S(1)} %bitcast.93), kind=kOutput, calls=%fused_computation.7 | convolution fusion | flops 10875174912 | bytes 20054016 | tf_op jit(solution)/shard_map/dot_general | solution.py:54
  434.9 11.4 %copy.59 = bf16[4,288,3072]{2,0,1:T(4,128)(2,1)} copy(bf16[4,288,3072]{2,1,0:T(8,128)(2,1)} %bitcast.86) | data formatting | bytes 14155776 | tf_op jit(solution)/shard_map/reshape | solution.py:57
  446.3 7.6 %all-to-all-start.2 = ((bf16[4,288,3072]{2,0,1:T(4,128)(2,1)}), bf16[4,288,3072]{2,0,1:T(4,128)(2,1)}, u32[]{:S(2)}, u32[]{:S(2)}) async-start(bf16[4,288,3072]{2,0,1:T(4,128)(2,1)} %copy.59), calls=%async_computation.2 | async-start | bytes 14155776 | tf_op jit(solution)/shard_map/all_to_all | solution.py:58
  453.9 76.3 %all-to-all-done.2 = bf16[4,288,3072]{2,0,1:T(4,128)(2,1)} async-done(((bf16[4,288,3072]{2,0,1:T(4,128)(2,1)}), bf16[4,288,3072]{2,0,1:T(4,128)(2,1)}, u32[]{:S(2)}, u32[]{:S(2)}) %all-to-all-start.2) | async-done | bytes 7077920 | tf_op jit(solution)/shard_map/all_to_all | solution.py:58
  530.2 9.7 %copy.60 = bf16[8,4,36,3072]{3,1,0,2:T(4,128)(2,1)} copy(bf16[8,4,36,3072]{3,1,2,0:T(4,128)(2,1)} %bitcast.16) | data formatting | bytes 14155776 | tf_op jit(solution)/shard_map/all_to_all | solution.py:58
  539.9 19.1 %reshape.80 = bf16[32,36,3,16,64]{4,3,2,0,1:T(8,128)(2,1)} reshape(bf16[8,4,36,3072]{3,1,0,2:T(4,128)(2,1)} %copy.60) | data formatting | bytes 14155776 | tf_op jit(solution)/shard_map/reshape | solution.py:60
  559.0 9.4 %fusion.33 = (bf16[32,36,1,16,64]{4,3,2,0,1:T(8,128)(2,1)}, bf16[32,36,1,16,64]{4,3,2,0,1:T(8,128)(2,1)S(1)}, bf16[32,36,1,16,64]{4,3,2,0,1:T(8,128)(2,1)S(1)}) fusion(bf16[32,36,3,16,64]{4,3,2,0,1:T(8,128)(2,1)} %reshape.80), kind=kLoop, calls=%fused_computation.58 | loop fusion | bytes 14155776 | tf_op jit(solution)/shard_map/slice | solution.py:71
  568.4 5.2 fusion.17
  573.7 13.8 %fusion.35 = (f32[36,16,32]{2,1,0:T(8,128)S(1)}, f32[36,16,32,32]{2,3,1,0:T(8,128)}) fusion(f32[36,16,32,32]{2,3,1,0:T(8,128)} %fusion.17, pred[32]{0:T(512)(128)(4,1)S(1)} %iota_compare_fusion), kind=kOutput, calls=%fused_computation.60 | output fusion | flops 3538975 | bytes 4792352 | tf_op jit(solution)/shard_map/sub | solution.py:69
  587.5 9.6 %convert_bitcast_fusion = bf16[32,36,16,64]{3,0,2,1:T(8,128)(2,1)} fusion(f32[36,16,32,32]{2,3,1,0:T(8,128)} %get-tuple-element.11, f32[36,16,32]{2,1,0:T(8,128)S(1)} %get-tuple-element.10, bf16[32,36,1,16,64]{4,3,2,0,1:T(8,128)(2,1)} %get-tuple-element.5), kind=kOutput, calls=%fused_computation.34 | convolution fusion | flops 77856768 | bytes 7151616 | tf_op jit(solution)/shard_map/phfg,gphd->fphd/dot_general | solution.py:70
  597.1 6.3 copy.74
  603.4 7.5 %reshape.84 = bf16[32,36,1024]{2,1,0:T(8,128)(2,1)} reshape(bf16[32,36,16,64]{3,2,1,0:T(8,128)(2,1)} %copy.74) | data formatting | bytes 4718592 | tf_op jit(solution)/shard_map/reshape | solution.py:73
  610.8 37.8 %all_to_all.61 = bf16[32,36,1024]{2,1,0:T(8,128)(2,1)S(1)} all-to-all(bf16[32,36,1024]{2,1,0:T(8,128)(2,1)} %reshape.84), channel_id=1, replica_groups=mesh['tm'=8,'space'=4] {'tm'}, dimensions={0} | all-to-all | bytes 4718592 | tf_op jit(solution)/shard_map/all_to_all | solution.py:74
  648.7 1.8 copy.76
  650.5 0.0 copy-done.4
  650.5 0.0 copy-done.6
  650.5 5.4 fusion.15
  (13 shorter events, 0.1 us)
Async XLA Ops:
  0.0 414.3 %copy-start = (bf16[1024,1536]{1,0:T(8,128)(2,1)S(1)}, bf16[1024,1536]{1,0:T(8,128)(2,1)}, u32[]{:S(2)}) copy-start(bf16[1024,1536]{1,0:T(8,128)(2,1)} %param.9) | copy-start | bytes 9437188
  0.0 6.6 copy-start.1
  0.0 7.4 %copy-start.5 = (bf16[1536,3072]{1,0:T(8,128)(2,1)S(1)}, bf16[1536,3072]{1,0:T(8,128)(2,1)}, u32[]{:S(2)}) copy-start(bf16[1536,3072]{1,0:T(8,128)(2,1)} %param.8) | copy-start | bytes 28311556
  356.3 55.6 %all-to-all-start.1 = ((bf16[4,1152,256]{2,0,1:T(4,128)(2,1)}), bf16[4,1152,256]{2,0,1:T(4,128)(2,1)}, u32[]{:S(2)}, u32[]{:S(2)}) async-start(bf16[4,1152,256]{2,0,1:T(4,128)(2,1)} %copy.56), calls=%async_computation.1 | async-start | bytes 4718592 | tf_op jit(solution)/shard_map/all_to_all | solution.py:33
  411.8 2.7 copy-start.2
  414.3 7.4 %slice-start = ((s8[9437184]{0:T(1024)(128)(4,1)}), s8[4194304]{0:T(1024)(128)(4,1)S(1)}, s32[]{:S(2)}) async-start(s8[9437184]{0:T(1024)(128)(4,1)} %bitcast.92), calls=%async_computation.4 | async-start | bytes 8388608
  414.6 7.1 %slice-start.1 = ((s8[9437184]{0:T(1024)(128)(4,1)}), s8[4194304]{0:T(1024)(128)(4,1)S(1)}, s32[]{:S(2)}) async-start(s8[9437184]{0:T(1024)(128)(4,1)} %bitcast.92), calls=%async_computation.5 | async-start | bytes 8388608
  414.6 7.1 %slice-start.2 = ((s8[9437184]{0:T(1024)(128)(4,1)}), s8[1048576]{0:T(1024)(128)(4,1)S(1)}, s32[]{:S(2)}) async-start(s8[9437184]{0:T(1024)(128)(4,1)} %bitcast.92), calls=%async_computation.6 | async-start | bytes 2097152
  419.0 1.8 copy-start.3
  446.3 83.9 %all-to-all-start.2 = ((bf16[4,288,3072]{2,0,1:T(4,128)(2,1)}), bf16[4,288,3072]{2,0,1:T(4,128)(2,1)}, u32[]{:S(2)}, u32[]{:S(2)}) async-start(bf16[4,288,3072]{2,0,1:T(4,128)(2,1)} %copy.59), calls=%async_computation.2 | async-start | bytes 14155776 | tf_op jit(solution)/shard_map/all_to_all | solution.py:58
  610.8 39.7 %copy-start.4 = (bf16[4,288,1536]{2,1,0:T(8,128)(2,1)S(1)}, bf16[4,288,1536]{2,1,0:T(8,128)(2,1)}, u32[]{:S(2)}) copy-start(bf16[4,288,1536]{2,1,0:T(8,128)(2,1)} %copy-done.3) | copy-start | bytes 10616836
  610.8 39.7 %copy-start.6 = (bf16[1024,1536]{1,0:T(8,128)(2,1)S(1)}, bf16[1024,1536]{1,0:T(8,128)(2,1)}, u32[]{:S(2)}) copy-start(bf16[1024,1536]{1,0:T(8,128)(2,1)} %param.11) | copy-start | bytes 9437188
where the time goes:
time: 668 us; the launch traced here: 656 us
  blocking collectives  246 us (37%)
  local copies, waits for them, and re-layouts  136 us (20%)
  waiting for transfers between devices  126 us (19%)
  matrix products  111 us (17%)
  other arithmetic  23.2 us (3%)
  starting transfers between devices  13.1 us (2%)
    all_to_all x1, blocking collectives, per_device(): lax.all_to_all(qkv1, 'space', split_axis=3, concat_axis=1, tiled=True)  209 us
    all_to_all x1, waiting for transfers between devices, per_device(): lax.all_to_all(qkv2, 'tm', split_axis=1, concat_axis=0, tiled=True)  76.3 us
    all_to_all x1, waiting for transfers between devices, spatial_attend(): lax.all_to_all(result, 'space', split_axis=1, concat_axis=2, tiled=True)  49.4 us
    reshape x2, local copies, waits for them, and re-layouts, per_device(): qkv1 = qkv1.astype(jnp.bfloat16).reshape(frames, patches, 3, H * HD)  39.5 us
    all_to_all x1, blocking collectives, per_device(): lax.all_to_all(temporal, 'tm', split_axis=0, concat_axis=1, tiled=True)  37.8 us
    dot_general x1, matrix products, spatial_attend(): jnp.einsum('fhqk,fkhd->fqhd', weights, parts[:, :, 2], preferred_element_...  35 us
    sub x1, matrix products, spatial_attend(): weights = jax.nn.softmax(scores, axis=-1).astype(jnp.bfloat16)  25 us
    reshape x2, local copies, waits for them, and re-layouts, spatial_attend(): parts = items.reshape(count, total, 3, local_heads, HD)  22.5 us
  transfers between devices with their start and end apart: 2, of which 2 were waited for; matrix products, arithmetic and copies ran while one was open for 0% of the time, Pallas kernels for 0%

commit v1 on v0

--- a/solution.py
+++ b/solution.py
@@ -1,10 +1,19 @@
+import functools
+import math
+
 import jax
 import jax.numpy as jnp
 from jax import lax
+from jax.experimental import pallas as pl
+from jax.experimental.pallas import tpu as pltpu
 from jax.sharding import PartitionSpec as P
 
 H = 16
 HD = 64
+BF = jnp.bfloat16
+F32 = jnp.float32
+VMEM_LIMIT = 56 * 1024 * 1024
+LOG2E = 1.0 / math.log(2.0)
 
 
 def layer_norm(values):
@@ -33,7 +42,7 @@
     return lax.all_to_all(result, "space", split_axis=1, concat_axis=2, tiled=True)
 
 
-def per_device(video, frame_count, qkv_space, out_space, qkv_time, out_time):
+def general(video, frame_count, qkv_space, out_space, qkv_time, out_time):
     frames, patches, width = video.shape
     first = lax.axis_index("tm") * frames
     limit = frame_count[0]
@@ -80,6 +89,239 @@
     )
 
 
+def pair_softmax(query, key, value, low, mask, rows):
+    query = (query.astype(F32) * (0.125 * LOG2E)).astype(BF)
+    zero, one = jnp.zeros_like(query), jnp.ones_like(value)
+    queries = (jnp.where(low, query, zero), jnp.where(low, zero, query))
+    values = (jnp.where(low, value, one), jnp.where(low, one, value))
+    total = query.shape[0]
+    out = []
+    for start in range(0, total, rows):
+        sums = []
+        for head in range(2):
+            scores = lax.dot_general(
+                queries[head][start : start + rows],
+                key,
+                (((1,), (1,)), ((), ())),
+                preferred_element_type=F32,
+            )
+            if mask is not None:
+                scores = jnp.where(mask, scores, -1e30)
+            top = jnp.max(scores, axis=1, keepdims=True)
+            weights = jnp.exp2((scores - top).astype(BF))
+            sums.append(jnp.dot(weights, values[head], preferred_element_type=F32))
+        half = low[start : start + rows]
+        result = jnp.where(half, sums[0], sums[1])
+        norm = pltpu.roll(jnp.where(half, sums[1], sums[0]), HD, 1)
+        out.append((result / norm).astype(BF))
+    return out
+
+
+def norm_rows(wide):
+    center = wide - jnp.mean(wide, axis=-1, keepdims=True)
+    spread = jnp.mean(center * center, axis=-1, keepdims=True)
+    return (center * lax.rsqrt(spread + 1e-06)).astype(BF)
+
+
+def space_kernel(rows, x_ref, wq_ref, wk_ref, wv_ref, out_ref, norm_ref):
+    total = x_ref.shape[0]
+
+    @pl.when(pl.program_id(0) == 0)
+    def _():
+        @pl.loop(0, total // 96)
+        def _(i):
+            part = pl.ds(pl.multiple_of(i * 96, 96), 96)
+            norm_ref[part, :] = norm_rows(x_ref[part, :].astype(F32))
+
+    normed = norm_ref[...]
+    query = jnp.dot(normed, wq_ref[...], preferred_element_type=F32).astype(BF)
+    key = jnp.dot(normed, wk_ref[...], preferred_element_type=F32).astype(BF)
+    value = jnp.dot(normed, wv_ref[...], preferred_element_type=F32).astype(BF)
+    low = lax.broadcasted_iota(jnp.int32, (total, 2 * HD), 1) < HD
+    for pair in range(query.shape[1] // (2 * HD)):
+        cols = slice(pair * 2 * HD, (pair + 1) * 2 * HD)
+        out = pair_softmax(query[:, cols], key[:, cols], value[:, cols], low, None, rows)
+        for i, block in enumerate(out):
+            out_ref[i * rows : (i + 1) * rows, cols] = block
+
+
+def space_attention(frame, weights):
+    total, width = frame.shape
+    groups = 4
+    cols = H * HD // groups
+    return pl.pallas_call(
+        functools.partial(space_kernel, 288),
+        grid=(groups,),
+        in_specs=[
+            pl.BlockSpec((total, width), lambda i: (0, 0)),
+            pl.BlockSpec((width, cols), lambda i: (0, i)),
+            pl.BlockSpec((width, cols), lambda i: (0, groups + i)),
+            pl.BlockSpec((width, cols), lambda i: (0, 2 * groups + i)),
+        ],
+        out_specs=pl.BlockSpec((total, cols), lambda i: (0, i)),
+        out_shape=jax.ShapeDtypeStruct((total, H * HD), BF),
+        scratch_shapes=[pltpu.VMEM((total, width), BF)],
+        compiler_params=pltpu.CompilerParams(vmem_limit_bytes=VMEM_LIMIT),
+        cost_estimate=pl.CostEstimate(
+            flops=2 * total * width * 3 * H * HD + 4 * total * total * H * HD,
+            bytes_accessed=2 * (total * width + 3 * width * H * HD + total * H * HD),
+            transcendentals=total * total * H,
+        ),
+    )(frame, weights, weights, weights)
+
+
+def interleave(values):
+    frames, patches, width = values.shape
+    parts = values.reshape(frames, patches // 8, 8, width)
+    pieces = []
+    for half in range(2):
+        for f in range(frames):
+            pieces.append(parts[f][:, half * 4 : half * 4 + 4])
+    return jnp.concatenate(pieces, axis=1).reshape(frames * patches, width)
+
+
+def deinterleave(values, frames):
+    rows, width = values.shape
+    parts = values.reshape(rows // (8 * frames), 8 * frames, width)
+    out = []
+    for f in range(frames):
+        first = parts[:, f * 4 : f * 4 + 4]
+        second = parts[:, 4 * frames + f * 4 : 4 * frames + f * 4 + 4]
+        out.append(jnp.concatenate([first, second], axis=1).reshape(rows // frames, width))
+    return out
+
+
+def middle_kernel(count_ref, x_ref, s_ref, w_ref, out_ref):
+    frames, patches, width = x_ref.shape
+    branch = jnp.dot(
+        s_ref[...].reshape(frames * patches, s_ref.shape[2]), w_ref[...], preferred_element_type=F32
+    ).reshape(frames, patches, width)
+    first = lax.axis_index("tm") * frames
+    parts = []
+    for f in range(frames):
+        valid = (first + f < count_ref[0]).astype(F32)
+        parts.append(x_ref[f].astype(F32) + valid * branch[f])
+    out_ref[...] = interleave(jnp.stack(parts)).astype(BF)
+
+
+def middle_rows(frame_count, video, spatial, weights):
+    frames, patches, width = video.shape
+    step = 96
+    return pl.pallas_call(
+        middle_kernel,
+        grid=(patches // step,),
+        in_specs=[
+            pl.BlockSpec(memory_space=pltpu.SMEM),
+            pl.BlockSpec((frames, step, width), lambda i: (0, i, 0)),
+            pl.BlockSpec((frames, step, H * HD), lambda i: (0, i, 0)),
+            pl.BlockSpec((H * HD, width), lambda i: (0, 0)),
+        ],
+        out_specs=pl.BlockSpec((frames * step, width), lambda i: (i, 0)),
+        out_shape=jax.ShapeDtypeStruct((frames * patches, width), BF),
+        compiler_params=pltpu.CompilerParams(vmem_limit_bytes=VMEM_LIMIT),
+    )(frame_count, video, spatial, weights)
+
+
+def time_kernel(count_ref, x_ref, w_ref, out_ref):
+    sources, groups, rows, width = x_ref.shape
+    total = sources * rows
+    normed = jnp.concatenate(
+        [norm_rows(x_ref[:, g].reshape(total, width).astype(F32)) for g in range(groups)], axis=0
+    )
+    qkv = jnp.dot(normed, w_ref[...], preferred_element_type=F32).astype(BF)
+    low = lax.broadcasted_iota(jnp.int32, (total, 2 * HD), 1) < HD
+    row = lax.broadcasted_iota(jnp.int32, (total, total), 0)
+    col = lax.broadcasted_iota(jnp.int32, (total, total), 1)
+    mask = (row % 4 == col % 4) & (col // 4 < count_ref[0])
+    for g in range(groups):
+        own = qkv[g * total : (g + 1) * total]
+        for pair in range(H // 2):
+            parts = [
+                own[:, k * H * HD + pair * 2 * HD : k * H * HD + (pair + 1) * 2 * HD]
+                for k in range(3)
+            ]
+            (result,) = pair_softmax(*parts, low, mask, total)
+            out_ref[:, g, :, pair * 2 * HD : (pair + 1) * 2 * HD] = result.reshape(
+                sources, rows, 2 * HD
+            )
+
+
+def time_attention(frame_count, middle, weights):
+    sources, groups, rows, width = middle.shape
+    step = 3
+    return pl.pallas_call(
+        time_kernel,
+        grid=(groups // step,),
+        in_specs=[
+            pl.BlockSpec(memory_space=pltpu.SMEM),
+            pl.BlockSpec((sources, step, rows, width), lambda i: (0, i, 0, 0)),
+            pl.BlockSpec((width, 3 * H * HD), lambda i: (0, 0)),
+        ],
+        out_specs=pl.BlockSpec((sources, step, rows, H * HD), lambda i: (0, i, 0, 0)),
+        out_shape=jax.ShapeDtypeStruct((sources, groups, rows, H * HD), BF),
+        compiler_params=pltpu.CompilerParams(vmem_limit_bytes=VMEM_LIMIT),
+    )(frame_count, middle, weights)
+
+
+def final_kernel(count_ref, m_ref, t_ref, w_ref, out_ref):
+    frames, patches, width = out_ref.shape
+    branch = jnp.dot(t_ref[...], w_ref[...], preferred_element_type=F32)
+    first = lax.axis_index("tm") * frames
+    middles = deinterleave(m_ref[...].astype(F32), frames)
+    branches = deinterleave(branch, frames)
+    for f in range(frames):
+        valid = (first + f < count_ref[0]).astype(F32)
+        out_ref[f] = (middles[f] + valid * branches[f]).astype(BF)
+
+
+def final_rows(frame_count, middle, temporal, weights, frames):
+    rows, width = middle.shape
+    patches = rows // frames
+    step = 96
+    return pl.pallas_call(
+        final_kernel,
+        grid=(patches // step,),
+        in_specs=[
+            pl.BlockSpec(memory_space=pltpu.SMEM),
+            pl.BlockSpec((frames * step, width), lambda i: (i, 0)),
+            pl.BlockSpec((frames * step, H * HD), lambda i: (i, 0)),
+            pl.BlockSpec((H * HD, width), lambda i: (0, 0)),
+        ],
+        out_specs=pl.BlockSpec((frames, step, width), lambda i: (0, i, 0)),
+        out_shape=jax.ShapeDtypeStruct((frames, patches, width), BF),
+        compiler_params=pltpu.CompilerParams(vmem_limit_bytes=VMEM_LIMIT),
+    )(frame_count, middle, temporal, weights)
+
+
+def by_frame(video, frame_count, qkv_space, out_space, qkv_time, out_time):
+    frames, patches, width = video.shape
+    devices = lax.axis_size("tm")
+    frame = lax.all_to_all(video, "space", split_axis=0, concat_axis=0, tiled=True)
+    spatial = space_attention(frame.reshape(frames * patches, width), qkv_space)
+    spatial = spatial.reshape(frames, patches, H * HD)
+    spatial = lax.all_to_all(spatial, "space", split_axis=0, concat_axis=0, tiled=True)
+    middle = middle_rows(frame_count, video, spatial, out_space)
+    sent = middle.reshape(devices, frames * patches // devices, width)
+    sent = lax.all_to_all(sent, "tm", split_axis=0, concat_axis=0, tiled=True)
+    temporal = time_attention(frame_count, sent.reshape(devices, -1, 4 * frames, width), qkv_time)
+    temporal = temporal.reshape(devices, frames * patches // devices, H * HD)
+    temporal = lax.all_to_all(temporal, "tm", split_axis=0, concat_axis=0, tiled=True)
+    return final_rows(
+        frame_count, middle, temporal.reshape(frames * patches, H * HD), out_time, frames
+    )
+
+
+def per_device(video, *rest):
+    frames, patches, _ = video.shape
+    fits = (
+        frames == 4
+        and lax.axis_size("space") == frames
+        and lax.axis_size("tm") == 8
+        and patches == 288
+    )
+    return (by_frame if fits else general)(video, *rest)
+
+
 def solution(mesh):
     return jax.shard_map(
         per_device,

time: 668 us -> 353 us (0.53)
  local copies, waits for them, and re-layouts: 136 us -> 1.4 us
  Pallas kernels: 0 us -> 128 us
  matrix products: 111 us -> 0 us
  blocking collectives: 246 us -> 163 us
  waiting for transfers between devices: 126 us -> 49.3 us
  other arithmetic: 23.2 us -> 0 us
  starting transfers between devices: 13.1 us -> 5.06 us
    pallas_call x0 -> x4, Pallas kernels: none -> 128 us  [the longest x1 58.9 us: space_attention(): pl.pallas_call(functools.partial(space_kernel, 288), grid=(groups,), in_s...]
    reshape x9 -> x0, local copies, waits for them, and re-layouts: 111 us -> none  [the longest x2 39.5 us: per_device(): qkv1 = qkv1.astype(jnp.bfloat16).reshape(frames, patches, 3, H * HD)]
    dot_general x7 -> x0, matrix products: 85.9 us -> none  [the longest x1 35 us: spatial_attend(): jnp.einsum('fhqk,fkhd->fqhd', weights, parts[:, :, 2], preferred_element_...]
    all_to_all x2 -> x3, blocking collectives: 246 us -> 163 us  [the longest x1 82.3 us: by_frame(): lax.all_to_all(video, 'space', split_axis=0, concat_axis=0, tiled=True)]
    all_to_all x2 -> x1, waiting for transfers between devices: 126 us -> 49.3 us  [by_frame(): lax.all_to_all(spatial, 'space', split_axis=0, concat_axis=0, tiled=True)]
    sub x1 -> x0, matrix products: 25 us -> none  [spatial_attend(): weights = jax.nn.softmax(scores, axis=-1).astype(jnp.bfloat16)]
    sub x1 -> x0, other arithmetic: 13.8 us -> none  [per_device(): weights = jax.nn.softmax(scores, axis=-1).astype(jnp.bfloat16)]
    all_to_all x3 -> x0, local copies, waits for them, and re-layouts: 13.6 us -> none  [the longest x1 9.69 us: per_device(): lax.all_to_all(qkv2, 'tm', split_axis=1, concat_axis=0, tiled=True)]
  transfers between devices with their start and end apart: 2 -> 1, of which waited for: 2 -> 1; matrix products, arithmetic and copies ran while one was open for 0% -> 0% of each run, Pallas kernels for 0% -> 0%
where the time goes in v1:
time: 353 us; the launch traced here: 348 us
  blocking collectives  163 us (46%)
  Pallas kernels  128 us (36%)
  waiting for transfers between devices  49.3 us (14%)
  starting transfers between devices  5.06 us (1%)
    all_to_all x1, blocking collectives, by_frame(): lax.all_to_all(video, 'space', split_axis=0, concat_axis=0, tiled=True)  82.3 us
    pallas_call x1, Pallas kernels, space_attention(): pl.pallas_call(functools.partial(space_kernel, 288), grid=(groups,), in_s...  58.9 us
    pallas_call x1, Pallas kernels, time_attention(): pl.pallas_call(time_kernel, grid=(groups // step,), in_specs=[pl.BlockSpe...  51.8 us
    all_to_all x1, waiting for transfers between devices, by_frame(): lax.all_to_all(spatial, 'space', split_axis=0, concat_axis=0, tiled=True)  49.3 us
    all_to_all x1, blocking collectives, by_frame(): sent = lax.all_to_all(sent, 'tm', split_axis=0, concat_axis=0, tiled=True)  47.8 us
    all_to_all x1, blocking collectives, by_frame(): lax.all_to_all(temporal, 'tm', split_axis=0, concat_axis=0, tiled=True)  33.3 us
    pallas_call x1, Pallas kernels, final_rows(): pl.pallas_call(final_kernel, grid=(patches // step,), in_specs=[pl.BlockS...  8.69 us
    pallas_call x1, Pallas kernels, middle_rows(): pl.pallas_call(middle_kernel, grid=(patches // step,), in_specs=[pl.Block...  8.42 us
  transfers between devices with their start and end apart: 1, of which 1 were waited for; matrix products, arithmetic and copies ran while one was open for 0% of the time, Pallas kernels for 0%

profile of v1, /device:TPU:29, one launch (start us, length us, event | category | flops | bytes accessed | tf_op | source)
XLA Modules:
  0.0 347.7 jit_solution(18051629161463555029)
XLA Ops:
  0.0 82.3 %all_to_all.20 = bf16[4,288,1536]{2,1,0:T(8,128)(2,1)} all-to-all(bf16[4,288,1536]{2,1,0:T(8,128)(2,1)} %x_ref.1), channel_id=1, replica_groups=mesh['tm'=8,'space'=4] {'space'}, dimensions={0} | all-to-all | bytes 7077888 | tf_op jit(solution)/shard_map/all_to_all | solution.py:299
  82.3 58.9 %shard_map.64 = bf16[1152,1024]{1,0:T(8,128)(2,1)} custom-call(bf16[1152,1536]{1,0:T(8,128)(2,1)} %bitcast.10, bf16[1536,3072]{1,0:T(8,128)(2,1)} %wv_ref.1, bf16[1536,3072]{1,0:T(8,128)(2,1)} %wv_ref.1, bf16[1536,3072]{1,0:T(8,128)(2,1)} %wv_ref.1), custom_call_target="tpu_custom_call" | custom-call | flops 16307453952 | bytes 15335424 | tf_op jit(solution)/shard_map/pallas_call | solution.py:152
  141.2 5.1 %all-to-all-start.1 = ((bf16[4,288,1024]{2,1,0:T(8,128)(2,1)}), bf16[4,288,1024]{2,1,0:T(8,128)(2,1)S(1)}, u32[]{:S(2)}, u32[]{:S(2)}) async-start(bf16[4,288,1024]{2,1,0:T(8,128)(2,1)} %bitcast.11), calls=%async_computation.1 | async-start | bytes 4718592 | tf_op jit(solution)/shard_map/all_to_all | solution.py:302
  146.9 49.3 %all-to-all-done.1.s_ref = bf16[4,288,1024]{2,1,0:T(8,128)(2,1)S(1)} async-done(((bf16[4,288,1024]{2,1,0:T(8,128)(2,1)}), bf16[4,288,1024]{2,1,0:T(8,128)(2,1)S(1)}, u32[]{:S(2)}, u32[]{:S(2)}) %all-to-all-start.1) | async-done | bytes 2359328 | tf_op jit(solution)/shard_map/all_to_all | solution.py:302
  196.2 0.0 copy-start
  196.3 1.4 copy-done
  197.7 8.4 %shard_map.65.m_ref = bf16[1152,1536]{1,0:T(8,128)(2,1)} custom-call(s32[1]{0:T(128)S(6)} %copy.7.count_ref, bf16[4,288,1536]{2,1,0:T(8,128)(2,1)} %x_ref.1, bf16[4,288,1024]{2,1,0:T(8,128)(2,1)} %copy-done, bf16[1024,1536]{1,0:T(8,128)(2,1)} %w_ref.3), custom_call_target="tpu_custom_call" | custom-call | tf_op jit(solution)/shard_map/pallas_call | solution.py:210
  206.1 47.8 %all_to_all.21 = bf16[8,144,1536]{2,1,0:T(8,128)(2,1)} all-to-all(bf16[8,144,1536]{2,1,0:T(8,128)(2,1)} %bitcast.6), channel_id=1, replica_groups=mesh['tm'=8,'space'=4] {'tm'}, dimensions={0} | all-to-all | bytes 7077888 | tf_op jit(solution)/shard_map/all_to_all | solution.py:305
  253.9 51.8 %shard_map.66 = bf16[8,9,16,1024]{3,2,1,0:T(8,128)(2,1)} custom-call(s32[1]{0:T(128)S(6)} %copy.7.count_ref, bf16[8,9,16,1536]{3,2,1,0:T(8,128)(2,1)} %bitcast.7, bf16[1536,3072]{1,0:T(8,128)(2,1)} %w_ref.4), custom_call_target="tpu_custom_call" | custom-call | tf_op jit(solution)/shard_map/pallas_call | solution.py:252
  305.6 33.3 %all_to_all.22 = bf16[8,144,1024]{2,1,0:T(8,128)(2,1)} all-to-all(bf16[8,144,1024]{2,1,0:T(8,128)(2,1)} %bitcast.9), channel_id=1, replica_groups=mesh['tm'=8,'space'=4] {'tm'}, dimensions={0} | all-to-all | bytes 4718592 | tf_op jit(solution)/shard_map/all_to_all | solution.py:308
  339.0 8.7 %shard_map.67 = bf16[4,288,1536]{2,1,0:T(8,128)(2,1)} custom-call(s32[1]{0:T(128)S(6)} %copy.7.count_ref, bf16[1152,1536]{1,0:T(8,128)(2,1)} %shard_map.65.m_ref, bf16[1152,1024]{1,0:T(8,128)(2,1)} %bitcast.8, bf16[1024,1536]{1,0:T(8,128)(2,1)} %w_ref.5), custom_call_target="tpu_custom_call" | custom-call | tf_op jit(solution)/shard_map/pallas_call | solution.py:281
Async XLA Ops:
  141.2 55.0 %all-to-all-start.1 = ((bf16[4,288,1024]{2,1,0:T(8,128)(2,1)}), bf16[4,288,1024]{2,1,0:T(8,128)(2,1)S(1)}, u32[]{:S(2)}, u32[]{:S(2)}) async-start(bf16[4,288,1024]{2,1,0:T(8,128)(2,1)} %bitcast.11), calls=%async_computation.1 | async-start | bytes 4718592 | tf_op jit(solution)/shard_map/all_to_all | solution.py:302
  196.2 1.4 copy-start

commit v2 on v1

--- a/solution.py
+++ b/solution.py
@@ -89,85 +89,164 @@
     )
 
 
-def pair_softmax(query, key, value, low, mask, rows):
-    query = (query.astype(F32) * (0.125 * LOG2E)).astype(BF)
-    zero, one = jnp.zeros_like(query), jnp.ones_like(value)
-    queries = (jnp.where(low, query, zero), jnp.where(low, zero, query))
-    values = (jnp.where(low, value, one), jnp.where(low, one, value))
-    total = query.shape[0]
-    out = []
-    for start in range(0, total, rows):
-        sums = []
-        for head in range(2):
-            scores = lax.dot_general(
-                queries[head][start : start + rows],
-                key,
-                (((1,), (1,)), ((), ())),
-                preferred_element_type=F32,
-            )
-            if mask is not None:
-                scores = jnp.where(mask, scores, -1e30)
-            top = jnp.max(scores, axis=1, keepdims=True)
-            weights = jnp.exp2((scores - top).astype(BF))
-            sums.append(jnp.dot(weights, values[head], preferred_element_type=F32))
-        half = low[start : start + rows]
-        result = jnp.where(half, sums[0], sums[1])
-        norm = pltpu.roll(jnp.where(half, sums[1], sums[0]), HD, 1)
-        out.append((result / norm).astype(BF))
-    return out
-
-
 def norm_rows(wide):
     center = wide - jnp.mean(wide, axis=-1, keepdims=True)
     spread = jnp.mean(center * center, axis=-1, keepdims=True)
     return (center * lax.rsqrt(spread + 1e-06)).astype(BF)
 
 
-def space_kernel(rows, x_ref, wq_ref, wk_ref, wv_ref, out_ref, norm_ref):
-    total = x_ref.shape[0]
-
-    @pl.when(pl.program_id(0) == 0)
-    def _():
-        @pl.loop(0, total // 96)
+def space_kernel(video, weights, out, x_buf, w_buf, normed, qkv, sent, sems):
+    send_in, recv_in, local, send_out, recv_out, keep = sems
+    n, patches, width = x_buf.shape
+    chunks, _, _, cols = out.shape
+    me = lax.axis_index("space")
+    peers = [lax.rem(me + d, n) for d in range(n)]
+    froms = [lax.rem(me + n - d, n) for d in range(n)]
+
+    barrier = pltpu.get_barrier_semaphore()
+    for d in range(1, n):
+        pl.semaphore_signal(
+            barrier, inc=1, device_id={"space": peers[d]}, device_id_type=pl.DeviceIdType.MESH
+        )
+    own = pltpu.make_async_copy(video.at[me], x_buf.at[me], local.at[0])
+    own.start()
+    load = pltpu.make_async_copy(weights, w_buf, local.at[1])
+    load.start()
+    pl.semaphore_wait(barrier, n - 1)
+    arrivals = []
+    for d in range(1, n):
+        copy = pltpu.make_async_remote_copy(
+            src_ref=video.at[peers[d]],
+            dst_ref=x_buf.at[me],
+            send_sem=send_in.at[d],
+            recv_sem=recv_in.at[d],
+            device_id={"space": peers[d]},
+            device_id_type=pl.DeviceIdType.MESH,
+        )
+        copy.start()
+        arrivals.append(copy)
+    own.wait()
+    load.wait()
+
+    def project(source):
+        @pl.loop(0, patches // 96)
         def _(i):
             part = pl.ds(pl.multiple_of(i * 96, 96), 96)
-            norm_ref[part, :] = norm_rows(x_ref[part, :].astype(F32))
-
-    normed = norm_ref[...]
-    query = jnp.dot(normed, wq_ref[...], preferred_element_type=F32).astype(BF)
-    key = jnp.dot(normed, wk_ref[...], preferred_element_type=F32).astype(BF)
-    value = jnp.dot(normed, wv_ref[...], preferred_element_type=F32).astype(BF)
-    low = lax.broadcasted_iota(jnp.int32, (total, 2 * HD), 1) < HD
-    for pair in range(query.shape[1] // (2 * HD)):
-        cols = slice(pair * 2 * HD, (pair + 1) * 2 * HD)
-        out = pair_softmax(query[:, cols], key[:, cols], value[:, cols], low, None, rows)
-        for i, block in enumerate(out):
-            out_ref[i * rows : (i + 1) * rows, cols] = block
-
-
-def space_attention(frame, weights):
-    total, width = frame.shape
-    groups = 4
-    cols = H * HD // groups
+            normed[part, :] = norm_rows(x_buf[source, part, :].astype(F32))
+
+        start = pl.multiple_of(source * patches, patches)
+
+        @pl.loop(0, 6)
+        def _(i):
+            part = pl.ds(pl.multiple_of(i * 512, 512), 512)
+            result = jnp.dot(normed[...], w_buf[:, part], preferred_element_type=F32)
+            scale = jnp.where(i < 2, 0.125 * LOG2E, 1.0).astype(F32)
+            qkv[pl.ds(start, patches), part] = (result * scale).astype(BF)
+
+    project(me)
+    for d in range(1, n):
+        arrivals[d - 1].wait_recv()
+        project(froms[d])
+
+    low = lax.broadcasted_iota(jnp.int32, (patches, 2 * HD), 1) < HD
+    low_all = lax.broadcasted_iota(jnp.int32, (n * patches, 2 * HD), 1) < HD
+
+    def outgoing(c, d):
+        return pltpu.make_async_remote_copy(
+            src_ref=sent.at[c, d],
+            dst_ref=out.at[c, me],
+            send_sem=send_out.at[c, d],
+            recv_sem=recv_out.at[c, d],
+            device_id={"space": peers[d]},
+            device_id_type=pl.DeviceIdType.MESH,
+        )
+
+    @pl.loop(0, chunks)
+    def _(c):
+        keys, values = [], []
+        for pair in range(2):
+            start = pl.multiple_of(H * HD + c * cols + pair * 128, 128)
+            keys.append(qkv[:, pl.ds(start, 128)])
+            start = pl.multiple_of(2 * H * HD + c * cols + pair * 128, 128)
+            value = qkv[:, pl.ds(start, 128)]
+            one = jnp.ones_like(value)
+            values.append((jnp.where(low_all, value, one), jnp.where(low_all, one, value)))
+        units = [(d, pair, head) for d in (1, 2, 3, 0) for pair in range(2) for head in range(2)]
+
+        def scores_of(unit):
+            d, pair, head = unit
+            rows = pl.ds(pl.multiple_of(peers[d] * patches, patches), patches)
+            query = qkv[rows, pl.ds(pl.multiple_of(c * cols + pair * 128, 128), 128)]
+            zero = jnp.zeros_like(query)
+            query = jnp.where(low, query, zero) if head == 0 else jnp.where(low, zero, query)
+            return lax.dot_general(
+                query, keys[pair], (((1,), (1,)), ((), ())), preferred_element_type=F32
+            )
+
+        following = scores_of(units[0])
+        sums = []
+        for at, (d, pair, head) in enumerate(units):
+            scores = following
+            if at + 1 < len(units):
+                following = scores_of(units[at + 1])
+            top = jnp.max(scores, axis=1, keepdims=True)
+            exps = jnp.exp2((scores - top).astype(BF))
+            sums.append(jnp.dot(exps, values[pair][head], preferred_element_type=F32))
+            if head == 1:
+                result = jnp.where(low, sums[0], sums[1])
+                norm = pltpu.roll(jnp.where(low, sums[1], sums[0]), HD, 1)
+                sums = []
+                sent[c, d, :, pair * 128 : (pair + 1) * 128] = (result / norm).astype(BF)
+                if pair == 1:
+                    if d > 0:
+                        outgoing(c, d).start()
+                    else:
+                        pltpu.make_async_copy(sent.at[c, 0], out.at[c, me], keep.at[c]).start()
+
+    for copy in arrivals:
+        copy.wait_send()
+    for c in range(chunks):
+        pltpu.make_async_copy(sent.at[c, 0], out.at[c, me], keep.at[c]).wait()
+        for d in range(1, n):
+            outgoing(c, d).wait()
+
+
+def space_attention(video, weights):
+    n, patches, width = video.shape
+    total = n * patches
+    chunks = 4
+    cols = H * HD // chunks
+
+    def kernel(v, w, o, x_buf, w_buf, normed, qkv, sent, *sems):
+        space_kernel(v, w, o, x_buf, w_buf, normed, qkv, sent, sems)
+
     return pl.pallas_call(
-        functools.partial(space_kernel, 288),
-        grid=(groups,),
-        in_specs=[
-            pl.BlockSpec((total, width), lambda i: (0, 0)),
-            pl.BlockSpec((width, cols), lambda i: (0, i)),
-            pl.BlockSpec((width, cols), lambda i: (0, groups + i)),
-            pl.BlockSpec((width, cols), lambda i: (0, 2 * groups + i)),
+        kernel,
+        in_specs=[pl.BlockSpec(memory_space=pl.ANY)] * 2,
+        out_specs=pl.BlockSpec(memory_space=pl.ANY),
+        out_shape=jax.ShapeDtypeStruct((chunks, n, patches, cols), BF),
+        scratch_shapes=[
+            pltpu.VMEM((n, patches, width), BF),
+            pltpu.VMEM((width, 3 * H * HD), BF),
+            pltpu.VMEM((patches, width), BF),
+            pltpu.VMEM((total, 3 * H * HD), BF),
+            pltpu.VMEM((chunks, n, patches, cols), BF),
+            pltpu.SemaphoreType.DMA((n,)),
+            pltpu.SemaphoreType.DMA((n,)),
+            pltpu.SemaphoreType.DMA((2,)),
+            pltpu.SemaphoreType.DMA((chunks, n)),
+            pltpu.SemaphoreType.DMA((chunks, n)),
+            pltpu.SemaphoreType.DMA((chunks,)),
         ],
-        out_specs=pl.BlockSpec((total, cols), lambda i: (0, i)),
-        out_shape=jax.ShapeDtypeStruct((total, H * HD), BF),
-        scratch_shapes=[pltpu.VMEM((total, width), BF)],
-        compiler_params=pltpu.CompilerParams(vmem_limit_bytes=VMEM_LIMIT),
+        compiler_params=pltpu.CompilerParams(
+            vmem_limit_bytes=VMEM_LIMIT, collective_id=0, has_side_effects=True
+        ),
         cost_estimate=pl.CostEstimate(
             flops=2 * total * width * 3 * H * HD + 4 * total * total * H * HD,
             bytes_accessed=2 * (total * width + 3 * width * H * HD + total * H * HD),
             transcendentals=total * total * H,
         ),
-    )(frame, weights, weights, weights)
+    )(video, weights)
 
 
 def interleave(values):
@@ -193,8 +272,14 @@
 
 def middle_kernel(count_ref, x_ref, s_ref, w_ref, out_ref):
     frames, patches, width = x_ref.shape
-    branch = jnp.dot(
-        s_ref[...].reshape(frames * patches, s_ref.shape[2]), w_ref[...], preferred_element_type=F32
+    chunks, _, _, cols = s_ref.shape
+    branch = sum(
+        jnp.dot(
+            s_ref[c].reshape(frames * patches, cols),
+            w_ref[c * cols : (c + 1) * cols, :],
+            preferred_element_type=F32,
+        )
+        for c in range(chunks)
     ).reshape(frames, patches, width)
     first = lax.axis_index("tm") * frames
     parts = []
@@ -213,7 +298,7 @@
         in_specs=[
             pl.BlockSpec(memory_space=pltpu.SMEM),
             pl.BlockSpec((frames, step, width), lambda i: (0, i, 0)),
-            pl.BlockSpec((frames, step, H * HD), lambda i: (0, i, 0)),
+            pl.BlockSpec((spatial.shape[0], frames, step, spatial.shape[3]), lambda i: (0, 0, i, 0)),
             pl.BlockSpec((H * HD, width), lambda i: (0, 0)),
         ],
         out_specs=pl.BlockSpec((frames * step, width), lambda i: (i, 0)),
@@ -233,14 +318,31 @@
     row = lax.broadcasted_iota(jnp.int32, (total, total), 0)
     col = lax.broadcasted_iota(jnp.int32, (total, total), 1)
     mask = (row % 4 == col % 4) & (col // 4 < count_ref[0])
+    zero, one = jnp.zeros((total, 2 * HD), BF), jnp.ones((total, 2 * HD), BF)
     for g in range(groups):
         own = qkv[g * total : (g + 1) * total]
+        scores, values = [], []
         for pair in range(H // 2):
-            parts = [
+            query, key, value = [
                 own[:, k * H * HD + pair * 2 * HD : k * H * HD + (pair + 1) * 2 * HD]
                 for k in range(3)
             ]
-            (result,) = pair_softmax(*parts, low, mask, total)
+            query = (query.astype(F32) * (0.125 * LOG2E)).astype(BF)
+            values += [jnp.where(low, value, one), jnp.where(low, one, value)]
+            for masked in (jnp.where(low, query, zero), jnp.where(low, zero, query)):
+                scores.append(
+                    lax.dot_general(
+                        masked, key, (((1,), (1,)), ((), ())), preferred_element_type=F32
+                    )
+                )
+        scores = jnp.where(mask[None], jnp.stack(scores), -1e30)
+        top = jnp.max(scores, axis=2, keepdims=True)
+        exps = jnp.exp2((scores - top).astype(BF))
+        sums = [jnp.dot(exps[h], values[h], preferred_element_type=F32) for h in range(H)]
+        for pair in range(H // 2):
+            first, second = sums[2 * pair], sums[2 * pair + 1]
+            norm = pltpu.roll(jnp.where(low, second, first), HD, 1)
+            result = (jnp.where(low, first, second) / norm).astype(BF)
             out_ref[:, g, :, pair * 2 * HD : (pair + 1) * 2 * HD] = result.reshape(
                 sources, rows, 2 * HD
             )
@@ -296,10 +398,7 @@
 def by_frame(video, frame_count, qkv_space, out_space, qkv_time, out_time):
     frames, patches, width = video.shape
     devices = lax.axis_size("tm")
-    frame = lax.all_to_all(video, "space", split_axis=0, concat_axis=0, tiled=True)
-    spatial = space_attention(frame.reshape(frames * patches, width), qkv_space)
-    spatial = spatial.reshape(frames, patches, H * HD)
-    spatial = lax.all_to_all(spatial, "space", split_axis=0, concat_axis=0, tiled=True)
+    spatial = space_attention(video, qkv_space)
     middle = middle_rows(frame_count, video, spatial, out_space)
     sent = middle.reshape(devices, frames * patches // devices, width)
     sent = lax.all_to_all(sent, "tm", split_axis=0, concat_axis=0, tiled=True)

time: 353 us -> 259 us (0.73)
  blocking collectives: 163 us -> 80 us
  waiting for transfers between devices: 49.3 us -> 0 us
  Pallas kernels: 128 us -> 174 us
  starting transfers between devices: 5.06 us -> 0 us
    all_to_all x1 -> x0, blocking collectives: 82.3 us -> none  [by_frame(): lax.all_to_all(video, 'space', split_axis=0, concat_axis=0, tiled=True)]
    pallas_call x1, Pallas kernels: 58.9 us -> 133 us  [space_attention(): pl.pallas_call(kernel, in_specs=[pl.BlockSpec(memory_space=pl.ANY)] * 2,...]
    all_to_all x1 -> x0, waiting for transfers between devices: 49.3 us -> none  [by_frame(): lax.all_to_all(spatial, 'space', split_axis=0, concat_axis=0, tiled=True)]
    pallas_call x1, Pallas kernels: 51.8 us -> 23.6 us  [time_attention(): pl.pallas_call(time_kernel, grid=(groups // step,), in_specs=[pl.BlockSpe...]
    all_to_all x1 -> x0, starting transfers between devices: 5.06 us -> none  [by_frame(): lax.all_to_all(spatial, 'space', split_axis=0, concat_axis=0, tiled=True)]
  transfers between devices with their start and end apart: 1 -> 0, of which waited for: 1 -> 0; matrix products, arithmetic and copies ran while one was open for 0% -> 0% of each run, Pallas kernels for 0% -> 0%
where the time goes in v2:
time: 259 us; the launch traced here: 255 us
  Pallas kernels  174 us (67%)
  blocking collectives  80 us (31%)
    pallas_call x1, Pallas kernels, space_attention(): pl.pallas_call(kernel, in_specs=[pl.BlockSpec(memory_space=pl.ANY)] * 2,...  133 us
    all_to_all x1, blocking collectives, by_frame(): sent = lax.all_to_all(sent, 'tm', split_axis=0, concat_axis=0, tiled=True)  46.7 us
    all_to_all x1, blocking collectives, by_frame(): lax.all_to_all(temporal, 'tm', split_axis=0, concat_axis=0, tiled=True)  33.3 us
    pallas_call x1, Pallas kernels, time_attention(): pl.pallas_call(time_kernel, grid=(groups // step,), in_specs=[pl.BlockSpe...  23.6 us
    pallas_call x1, Pallas kernels, final_rows(): pl.pallas_call(final_kernel, grid=(patches // step,), in_specs=[pl.BlockS...  8.69 us
    pallas_call x1, Pallas kernels, middle_rows(): pl.pallas_call(middle_kernel, grid=(patches // step,), in_specs=[pl.Block...  8.62 us

profile of v2, /device:TPU:29, one launch (start us, length us, event | category | flops | bytes accessed | tf_op | source)
XLA Modules:
  0.0 255.0 jit_solution(6212535876049355902)
XLA Ops:
  0.7 133.4 %shard_map.64.s_ref = bf16[4,4,288,256]{3,2,1,0:T(8,128)(2,1)} custom-call(bf16[4,288,1536]{2,1,0:T(8,128)(2,1)} %x_ref.1, bf16[1536,3072]{1,0:T(8,128)(2,1)} %w.1), custom_call_target="tpu_custom_call" | custom-call | flops 16307453952 | bytes 15335424 | tf_op jit(solution)/shard_map/pallas_call | solution.py:223
  134.1 8.6 %shard_map.65.m_ref = bf16[1152,1536]{1,0:T(8,128)(2,1)} custom-call(s32[1]{0:T(128)S(6)} %copy.7.count_ref, bf16[4,288,1536]{2,1,0:T(8,128)(2,1)} %x_ref.1, bf16[4,4,288,256]{3,2,1,0:T(8,128)(2,1)} %shard_map.64.s_ref, bf16[1024,1536]{1,0:T(8,128)(2,1)} %w_ref.3), custom_call_target="tpu_custom_call" | custom-call | tf_op jit(solution)/shard_map/pallas_call | solution.py:295
  142.7 46.7 %all_to_all.10 = bf16[8,144,1536]{2,1,0:T(8,128)(2,1)} all-to-all(bf16[8,144,1536]{2,1,0:T(8,128)(2,1)} %bitcast.4), channel_id=1, replica_groups=mesh['tm'=8,'space'=4] {'tm'}, dimensions={0} | all-to-all | bytes 7077888 | tf_op jit(solution)/shard_map/all_to_all | solution.py:404
  189.4 23.6 %shard_map.66 = bf16[8,9,16,1024]{3,2,1,0:T(8,128)(2,1)} custom-call(s32[1]{0:T(128)S(6)} %copy.7.count_ref, bf16[8,9,16,1536]{3,2,1,0:T(8,128)(2,1)} %bitcast.5, bf16[1536,3072]{1,0:T(8,128)(2,1)} %w_ref.4), custom_call_target="tpu_custom_call" | custom-call | tf_op jit(solution)/shard_map/pallas_call | solution.py:354
  213.0 33.3 %all_to_all.11 = bf16[8,144,1024]{2,1,0:T(8,128)(2,1)} all-to-all(bf16[8,144,1024]{2,1,0:T(8,128)(2,1)} %bitcast.7), channel_id=1, replica_groups=mesh['tm'=8,'space'=4] {'tm'}, dimensions={0} | all-to-all | bytes 4718592 | tf_op jit(solution)/shard_map/all_to_all | solution.py:407
  246.3 8.7 %shard_map.67 = bf16[4,288,1536]{2,1,0:T(8,128)(2,1)} custom-call(s32[1]{0:T(128)S(6)} %copy.7.count_ref, bf16[1152,1536]{1,0:T(8,128)(2,1)} %shard_map.65.m_ref, bf16[1152,1024]{1,0:T(8,128)(2,1)} %bitcast.6, bf16[1024,1536]{1,0:T(8,128)(2,1)} %w_ref.5), custom_call_target="tpu_custom_call" | custom-call | tf_op jit(solution)/shard_map/pallas_call | solution.py:383

commit v3 on v2

--- a/solution.py
+++ b/solution.py
@@ -113,40 +113,44 @@
     load = pltpu.make_async_copy(weights, w_buf, local.at[1])
     load.start()
     pl.semaphore_wait(barrier, n - 1)
+    parts = patches // 96
     arrivals = []
-    for d in range(1, n):
-        copy = pltpu.make_async_remote_copy(
-            src_ref=video.at[peers[d]],
-            dst_ref=x_buf.at[me],
-            send_sem=send_in.at[d],
-            recv_sem=recv_in.at[d],
-            device_id={"space": peers[d]},
-            device_id_type=pl.DeviceIdType.MESH,
-        )
-        copy.start()
-        arrivals.append(copy)
+    for t in range(parts):
+        rows = pl.ds(t * 96, 96)
+        for d in range(1, n):
+            copy = pltpu.make_async_remote_copy(
+                src_ref=video.at[peers[d], rows],
+                dst_ref=x_buf.at[me, rows],
+                send_sem=send_in.at[t, d],
+                recv_sem=recv_in.at[t, d],
+                device_id={"space": peers[d]},
+                device_id_type=pl.DeviceIdType.MESH,
+            )
+            copy.start()
+            arrivals.append(copy)
     own.wait()
     load.wait()
 
-    def project(source):
-        @pl.loop(0, patches // 96)
-        def _(i):
-            part = pl.ds(pl.multiple_of(i * 96, 96), 96)
-            normed[part, :] = norm_rows(x_buf[source, part, :].astype(F32))
-
-        start = pl.multiple_of(source * patches, patches)
+    def project(pieces):
+        for at, (source, offset) in enumerate(pieces):
+            rows = x_buf[source, offset : offset + 96, :]
+            normed[at * 96 : (at + 1) * 96, :] = norm_rows(rows.astype(F32))
 
         @pl.loop(0, 6)
         def _(i):
             part = pl.ds(pl.multiple_of(i * 512, 512), 512)
             result = jnp.dot(normed[...], w_buf[:, part], preferred_element_type=F32)
             scale = jnp.where(i < 2, 0.125 * LOG2E, 1.0).astype(F32)
-            qkv[pl.ds(start, patches), part] = (result * scale).astype(BF)
-
-    project(me)
-    for d in range(1, n):
-        arrivals[d - 1].wait_recv()
-        project(froms[d])
+            result = (result * scale).astype(BF)
+            for at, (source, offset) in enumerate(pieces):
+                start = pl.multiple_of(source * patches + offset, 96)
+                qkv[pl.ds(start, 96), part] = result[at * 96 : (at + 1) * 96]
+
+    project([(me, t * 96) for t in range(parts)])
+    for t in range(parts):
+        for d in range(1, n):
+            arrivals[t * (n - 1) + d - 1].wait_recv()
+        project([(froms[d], t * 96) for d in range(1, n)])
 
     low = lax.broadcasted_iota(jnp.int32, (patches, 2 * HD), 1) < HD
     low_all = lax.broadcasted_iota(jnp.int32, (n * patches, 2 * HD), 1) < HD
@@ -231,8 +235,8 @@
             pltpu.VMEM((patches, width), BF),
             pltpu.VMEM((total, 3 * H * HD), BF),
             pltpu.VMEM((chunks, n, patches, cols), BF),
-            pltpu.SemaphoreType.DMA((n,)),
-            pltpu.SemaphoreType.DMA((n,)),
+            pltpu.SemaphoreType.DMA((patches // 96, n)),
+            pltpu.SemaphoreType.DMA((patches // 96, n)),
             pltpu.SemaphoreType.DMA((2,)),
             pltpu.SemaphoreType.DMA((chunks, n)),
             pltpu.SemaphoreType.DMA((chunks, n)),
@@ -270,56 +274,28 @@
     return out
 
 
-def middle_kernel(count_ref, x_ref, s_ref, w_ref, out_ref):
-    frames, patches, width = x_ref.shape
-    chunks, _, _, cols = s_ref.shape
-    branch = sum(
-        jnp.dot(
-            s_ref[c].reshape(frames * patches, cols),
-            w_ref[c * cols : (c + 1) * cols, :],
-            preferred_element_type=F32,
-        )
-        for c in range(chunks)
-    ).reshape(frames, patches, width)
-    first = lax.axis_index("tm") * frames
-    parts = []
-    for f in range(frames):
-        valid = (first + f < count_ref[0]).astype(F32)
-        parts.append(x_ref[f].astype(F32) + valid * branch[f])
-    out_ref[...] = interleave(jnp.stack(parts)).astype(BF)
-
-
-def middle_rows(frame_count, video, spatial, weights):
-    frames, patches, width = video.shape
-    step = 96
-    return pl.pallas_call(
-        middle_kernel,
-        grid=(patches // step,),
-        in_specs=[
-            pl.BlockSpec(memory_space=pltpu.SMEM),
-            pl.BlockSpec((frames, step, width), lambda i: (0, i, 0)),
-            pl.BlockSpec((spatial.shape[0], frames, step, spatial.shape[3]), lambda i: (0, 0, i, 0)),
-            pl.BlockSpec((H * HD, width), lambda i: (0, 0)),
-        ],
-        out_specs=pl.BlockSpec((frames * step, width), lambda i: (i, 0)),
-        out_shape=jax.ShapeDtypeStruct((frames * patches, width), BF),
-        compiler_params=pltpu.CompilerParams(vmem_limit_bytes=VMEM_LIMIT),
-    )(frame_count, video, spatial, weights)
-
-
-def time_kernel(count_ref, x_ref, w_ref, out_ref):
-    sources, groups, rows, width = x_ref.shape
+STEP = 96
+GROUPS = 3
+
+
+def time_rows(x, weights, count):
+    sources, every, width = x.shape
+    rows = every // GROUPS
     total = sources * rows
     normed = jnp.concatenate(
-        [norm_rows(x_ref[:, g].reshape(total, width).astype(F32)) for g in range(groups)], axis=0
-    )
-    qkv = jnp.dot(normed, w_ref[...], preferred_element_type=F32).astype(BF)
+        [
+            norm_rows(x[:, g * rows : (g + 1) * rows].reshape(total, width).astype(F32))
+            for g in range(GROUPS)
+        ],
+        axis=0,
+    )
+    qkv = jnp.dot(normed, weights[...], preferred_element_type=F32).astype(BF)
     low = lax.broadcasted_iota(jnp.int32, (total, 2 * HD), 1) < HD
     row = lax.broadcasted_iota(jnp.int32, (total, total), 0)
     col = lax.broadcasted_iota(jnp.int32, (total, total), 1)
-    mask = (row % 4 == col % 4) & (col // 4 < count_ref[0])
+    mask = (row % 4 == col % 4) & (col // 4 < count)
     zero, one = jnp.zeros((total, 2 * HD), BF), jnp.ones((total, 2 * HD), BF)
-    for g in range(groups):
+    for g in range(GROUPS):
         own = qkv[g * total : (g + 1) * total]
         scores, values = [], []
         for pair in range(H // 2):
@@ -343,71 +319,154 @@
             first, second = sums[2 * pair], sums[2 * pair + 1]
             norm = pltpu.roll(jnp.where(low, second, first), HD, 1)
             result = (jnp.where(low, first, second) / norm).astype(BF)
-            out_ref[:, g, :, pair * 2 * HD : (pair + 1) * 2 * HD] = result.reshape(
-                sources, rows, 2 * HD
+            yield g, pair, result.reshape(sources, rows, 2 * HD)
+
+
+def time_kernel(
+    count_ref, video, spatial, w_space, w_qkv, w_time, out, ws, wq, wt, middle, x_in, t_out, t_in, sems
+):
+    loads, send_a, recv_a, send_b, recv_b = sems
+    frames, patches, width = video.shape
+    chunks, n, share, _ = x_in.shape
+    pieces, cols = spatial.shape[0], spatial.shape[3]
+    me = lax.axis_index("tm")
+    peers = [lax.rem(me + d, n) for d in range(n)]
+    froms = [lax.rem(me + n - d, n) for d in range(n)]
+    count = count_ref[0]
+    valid = [(me * frames + f < count).astype(F32) for f in range(frames)]
+
+    barrier = pltpu.get_barrier_semaphore()
+    for d in range(1, n):
+        pl.semaphore_signal(
+            barrier, inc=1, device_id={"tm": peers[d]}, device_id_type=pl.DeviceIdType.MESH
+        )
+    copies = [
+        pltpu.make_async_copy(src, dst, loads.at[i])
+        for i, (src, dst) in enumerate(((w_space, ws), (w_qkv, wq), (w_time, wt)))
+    ]
+    for copy in copies:
+        copy.start()
+
+    def forth(k, d):
+        return pltpu.make_async_remote_copy(
+            src_ref=middle.at[k, peers[d]],
+            dst_ref=x_in.at[k, me],
+            send_sem=send_a.at[k, d],
+            recv_sem=recv_a.at[k, d],
+            device_id={"tm": peers[d]},
+            device_id_type=pl.DeviceIdType.MESH,
+        )
+
+    def back(k, d):
+        return pltpu.make_async_remote_copy(
+            src_ref=t_out.at[k, peers[d]],
+            dst_ref=t_in.at[k, me],
+            send_sem=send_b.at[k, d],
+            recv_sem=recv_b.at[k, d],
+            device_id={"tm": peers[d]},
+            device_id_type=pl.DeviceIdType.MESH,
+        )
+
+    pl.semaphore_wait(barrier, n - 1)
+    copies[0].wait()
+
+    @pl.loop(0, chunks)
+    def _(k):
+        part = pl.ds(pl.multiple_of(k * STEP, STEP), STEP)
+        branch = sum(
+            jnp.dot(
+                spatial[c, :, part, :].reshape(frames * STEP, cols),
+                ws[c * cols : (c + 1) * cols, :],
+                preferred_element_type=F32,
             )
-
-
-def time_attention(frame_count, middle, weights):
-    sources, groups, rows, width = middle.shape
-    step = 3
+            for c in range(pieces)
+        ).reshape(frames, STEP, width)
+        wide = [video[f, part, :].astype(F32) + valid[f] * branch[f] for f in range(frames)]
+        middle[k] = interleave(jnp.stack(wide)).astype(BF).reshape(n, share, width)
+        for d in range(1, n):
+            forth(k, d).start()
+        x_in[k, me] = middle[k, me]
+
+    copies[1].wait()
+
+    @pl.loop(0, chunks)
+    def _(k):
+        for d in range(1, n):
+            forth(k, d).wait_recv()
+        rows = share // GROUPS
+        for g, pair, result in time_rows(x_in[k], wq, count):
+            t_out[k, :, g * rows : (g + 1) * rows, pair * 2 * HD : (pair + 1) * 2 * HD] = result
+        for d in range(1, n):
+            back(k, d).start()
+        t_in[k, me] = t_out[k, me]
+
+    copies[2].wait()
+
+    @pl.loop(0, chunks)
+    def _(k):
+        for d in range(1, n):
+            back(k, d).wait_recv()
+        branch = jnp.dot(
+            t_in[k].reshape(n * share, H * HD), wt[...], preferred_element_type=F32
+        )
+        middles = deinterleave(middle[k].reshape(n * share, width).astype(F32), frames)
+        branches = deinterleave(branch, frames)
+        part = pl.ds(pl.multiple_of(k * STEP, STEP), STEP)
+        for f in range(frames):
+            out[f, part, :] = (middles[f] + valid[f] * branches[f]).astype(BF)
+
+    @pl.loop(0, chunks)
+    def _(k):
+        for d in range(1, n):
+            forth(k, d).wait_send()
+            back(k, d).wait_send()
+
+
+def time_part(frame_count, video, spatial, w_space, w_qkv, w_time):
+    frames, patches, width = video.shape
+    n = lax.axis_size("tm")
+    chunks = patches // STEP
+    share = frames * STEP // n
+
+    def kernel(*refs):
+        time_kernel(*refs[:14], refs[14:])
+
+    vmem = pl.BlockSpec(memory_space=pltpu.VMEM)
+    hbm = pl.BlockSpec(memory_space=pl.ANY)
+    tokens = frames * patches
     return pl.pallas_call(
-        time_kernel,
-        grid=(groups // step,),
-        in_specs=[
-            pl.BlockSpec(memory_space=pltpu.SMEM),
-            pl.BlockSpec((sources, step, rows, width), lambda i: (0, i, 0, 0)),
-            pl.BlockSpec((width, 3 * H * HD), lambda i: (0, 0)),
+        kernel,
+        in_specs=[pl.BlockSpec(memory_space=pltpu.SMEM), vmem, vmem, hbm, hbm, hbm],
+        out_specs=vmem,
+        out_shape=jax.ShapeDtypeStruct(video.shape, BF),
+        scratch_shapes=[
+            pltpu.VMEM(w_space.shape, BF),
+            pltpu.VMEM(w_qkv.shape, BF),
+            pltpu.VMEM(w_time.shape, BF),
+            pltpu.VMEM((chunks, n, share, width), BF),
+            pltpu.VMEM((chunks, n, share, width), BF),
+            pltpu.VMEM((chunks, n, share, H * HD), BF),
+            pltpu.VMEM((chunks, n, share, H * HD), BF),
+            pltpu.SemaphoreType.DMA((3,)),
+            pltpu.SemaphoreType.DMA((chunks, n)),
+            pltpu.SemaphoreType.DMA((chunks, n)),
+            pltpu.SemaphoreType.DMA((chunks, n)),
+            pltpu.SemaphoreType.DMA((chunks, n)),
         ],
-        out_specs=pl.BlockSpec((sources, step, rows, H * HD), lambda i: (0, i, 0, 0)),
-        out_shape=jax.ShapeDtypeStruct((sources, groups, rows, H * HD), BF),
-        compiler_params=pltpu.CompilerParams(vmem_limit_bytes=VMEM_LIMIT),
-    )(frame_count, middle, weights)
-
-
-def final_kernel(count_ref, m_ref, t_ref, w_ref, out_ref):
-    frames, patches, width = out_ref.shape
-    branch = jnp.dot(t_ref[...], w_ref[...], preferred_element_type=F32)
-    first = lax.axis_index("tm") * frames
-    middles = deinterleave(m_ref[...].astype(F32), frames)
-    branches = deinterleave(branch, frames)
-    for f in range(frames):
-        valid = (first + f < count_ref[0]).astype(F32)
-        out_ref[f] = (middles[f] + valid * branches[f]).astype(BF)
-
-
-def final_rows(frame_count, middle, temporal, weights, frames):
-    rows, width = middle.shape
-    patches = rows // frames
-    step = 96
-    return pl.pallas_call(
-        final_kernel,
-        grid=(patches // step,),
-        in_specs=[
-            pl.BlockSpec(memory_space=pltpu.SMEM),
-            pl.BlockSpec((frames * step, width), lambda i: (i, 0)),
-            pl.BlockSpec((frames * step, H * HD), lambda i: (i, 0)),
-            pl.BlockSpec((H * HD, width), lambda i: (0, 0)),
-        ],
-        out_specs=pl.BlockSpec((frames, step, width), lambda i: (0, i, 0)),
-        out_shape=jax.ShapeDtypeStruct((frames, patches, width), BF),
-        compiler_params=pltpu.CompilerParams(vmem_limit_bytes=VMEM_LIMIT),
-    )(frame_count, middle, temporal, weights)
+        compiler_params=pltpu.CompilerParams(
+            vmem_limit_bytes=VMEM_LIMIT, collective_id=1, has_side_effects=True
+        ),
+        cost_estimate=pl.CostEstimate(
+            flops=2 * tokens * width * 5 * H * HD + 4 * tokens * 128 * H * HD,
+            bytes_accessed=2 * (2 * tokens * width + tokens * H * HD + 5 * width * H * HD),
+            transcendentals=tokens * 128 * H,
+        ),
+    )(frame_count, video, spatial, w_space, w_qkv, w_time)
 
 
 def by_frame(video, frame_count, qkv_space, out_space, qkv_time, out_time):
-    frames, patches, width = video.shape
-    devices = lax.axis_size("tm")
     spatial = space_attention(video, qkv_space)
-    middle = middle_rows(frame_count, video, spatial, out_space)
-    sent = middle.reshape(devices, frames * patches // devices, width)
-    sent = lax.all_to_all(sent, "tm", split_axis=0, concat_axis=0, tiled=True)
-    temporal = time_attention(frame_count, sent.reshape(devices, -1, 4 * frames, width), qkv_time)
-    temporal = temporal.reshape(devices, frames * patches // devices, H * HD)
-    temporal = lax.all_to_all(temporal, "tm", split_axis=0, concat_axis=0, tiled=True)
-    return final_rows(
-        frame_count, middle, temporal.reshape(frames * patches, H * HD), out_time, frames
-    )
+    return time_part(frame_count, video, spatial, out_space, qkv_time, out_time)
 
 
 def per_device(video, *rest):

time: 259 us -> 217 us (0.84); the launches traced: 255 us -> 217 us
  blocking collectives: 80 us -> 0 us
  Pallas kernels: 174 us -> 212 us
  local copies, waits for them, and re-layouts: 0 us -> 4.02 us
    all_to_all x2 -> x0, blocking collectives: 80 us -> none  [the longest x1 46.7 us: by_frame(): sent = lax.all_to_all(sent, 'tm', split_axis=0, concat_axis=0, tiled=True)]
    pallas_call x3 -> x1, Pallas kernels: 40.9 us -> 76 us  [time_part(): pl.pallas_call(kernel, in_specs=[pl.BlockSpec(memory_space=pltpu.SMEM), v...]
    unnamed x0 -> x1, local copies, waits for them, and re-layouts: none -> 4.02 us
    pallas_call x1, Pallas kernels: 133 us -> 136 us  [space_attention(): pl.pallas_call(kernel, in_specs=[pl.BlockSpec(memory_space=pl.ANY)] * 2,...]
where the time goes in v3:
time: 217 us
  Pallas kernels  212 us (98%)
  local copies, waits for them, and re-layouts  4.02 us (2%)
    pallas_call x1, Pallas kernels, space_attention(): pl.pallas_call(kernel, in_specs=[pl.BlockSpec(memory_space=pl.ANY)] * 2,...  136 us
    pallas_call x1, Pallas kernels, time_part(): pl.pallas_call(kernel, in_specs=[pl.BlockSpec(memory_space=pltpu.SMEM), v...  76 us

profile of v3, /device:TPU:29, one launch (start us, length us, event | category | flops | bytes accessed | tf_op | source)
XLA Modules:
  0.0 217.1 jit_solution(6568131153912971072)
XLA Ops:
  0.7 136.4 %shard_map.64.refs_2_ = bf16[4,4,288,256]{3,2,1,0:T(8,128)(2,1)} custom-call(bf16[4,288,1536]{2,1,0:T(8,128)(2,1)} %refs_1_.1, bf16[1536,3072]{1,0:T(8,128)(2,1)} %w.1), custom_call_target="tpu_custom_call" | custom-call | flops 16307453952 | bytes 15335424 | tf_op jit(solution)/shard_map/pallas_call | solution.py:227
  137.1 76.0 %shard_map.65 = bf16[4,288,1536]{2,1,0:T(8,128)(2,1)} custom-call(s32[1]{0:T(128)S(6)} %copy.8.refs_0_, bf16[4,288,1536]{2,1,0:T(8,128)(2,1)} %refs_1_.1, bf16[4,4,288,256]{3,2,1,0:T(8,128)(2,1)} %shard_map.64.refs_2_, bf16[1024,1536]{1,0:T(8,128)(2,1)} %refs_3_.1, bf16[1536,3072]{1,0:T(8,128)(2,1)} %refs_4_.1, bf16[1024,1536]{1,0:T(8,128)(2,1)} %refs_5_.1), custom_call_target="tpu_custom_call" | custom-call | flops 18723373056 | bytes 25165824 | tf_op jit(solution)/shard_map/pallas_call | solution.py:437
  213.1 4.0 %copy.9 = bf16[4,288,1536]{2,1,0:T(8,128)(2,1)} copy(bf16[4,288,1536]{2,1,0:T(8,128)(2,1)} %shard_map.65) | data formatting | bytes 7077888

commit v4 on v0

--- a/solution.py
+++ b/solution.py
@@ -1,10 +1,18 @@
+import math
+
 import jax
 import jax.numpy as jnp
 from jax import lax
+from jax.experimental import pallas as pl
+from jax.experimental.pallas import tpu as pltpu
 from jax.sharding import PartitionSpec as P
 
 H = 16
 HD = 64
+BF = jnp.bfloat16
+F32 = jnp.float32
+VMEM_LIMIT = 62 * 1024 * 1024
+LOG2E = 1.0 / math.log(2.0)
 
 
 def layer_norm(values):
@@ -33,7 +41,7 @@
     return lax.all_to_all(result, "space", split_axis=1, concat_axis=2, tiled=True)
 
 
-def per_device(video, frame_count, qkv_space, out_space, qkv_time, out_time):
+def general(video, frame_count, qkv_space, out_space, qkv_time, out_time):
     frames, patches, width = video.shape
     first = lax.axis_index("tm") * frames
     limit = frame_count[0]
@@ -80,6 +88,347 @@
     )
 
 
+def norm_rows(wide):
+    center = wide - jnp.mean(wide, axis=-1, keepdims=True)
+    spread = jnp.mean(center * center, axis=-1, keepdims=True)
+    return (center * lax.rsqrt(spread + 1e-06)).astype(BF)
+
+
+def interleave(values):
+    frames, patches, width = values.shape
+    parts = values.reshape(frames, patches // 8, 8, width)
+    pieces = []
+    for half in range(2):
+        for f in range(frames):
+            pieces.append(parts[f][:, half * 4 : half * 4 + 4])
+    return jnp.concatenate(pieces, axis=1).reshape(frames * patches, width)
+
+
+def deinterleave(values, frames):
+    rows, width = values.shape
+    parts = values.reshape(rows // (8 * frames), 8 * frames, width)
+    out = []
+    for f in range(frames):
+        first = parts[:, f * 4 : f * 4 + 4]
+        second = parts[:, 4 * frames + f * 4 : 4 * frames + f * 4 + 4]
+        out.append(jnp.concatenate([first, second], axis=1).reshape(rows // frames, width))
+    return out
+
+
+STEP = 96
+GROUPS = 3
+
+
+def time_rows(x, weights, count):
+    sources, every, width = x.shape
+    rows = every // GROUPS
+    total = sources * rows
+    normed = jnp.concatenate(
+        [
+            norm_rows(x[:, g * rows : (g + 1) * rows].reshape(total, width).astype(F32))
+            for g in range(GROUPS)
+        ],
+        axis=0,
+    )
+    qkv = jnp.dot(normed, weights[...], preferred_element_type=F32).astype(BF)
+    low = lax.broadcasted_iota(jnp.int32, (total, 2 * HD), 1) < HD
+    row = lax.broadcasted_iota(jnp.int32, (total, total), 0)
+    col = lax.broadcasted_iota(jnp.int32, (total, total), 1)
+    mask = (row % 4 == col % 4) & (col // 4 < count)
+    zero, one = jnp.zeros((total, 2 * HD), BF), jnp.ones((total, 2 * HD), BF)
+    for g in range(GROUPS):
+        own = qkv[g * total : (g + 1) * total]
+        scores, values = [], []
+        for pair in range(H // 2):
+            query, key, value = [
+                own[:, k * H * HD + pair * 2 * HD : k * H * HD + (pair + 1) * 2 * HD]
+                for k in range(3)
+            ]
+            query = (query.astype(F32) * (0.125 * LOG2E)).astype(BF)
+            values += [jnp.where(low, value, one), jnp.where(low, one, value)]
+            for masked in (jnp.where(low, query, zero), jnp.where(low, zero, query)):
+                scores.append(
+                    lax.dot_general(
+                        masked, key, (((1,), (1,)), ((), ())), preferred_element_type=F32
+                    )
+                )
+        scores = jnp.where(mask[None], jnp.stack(scores), -1e30)
+        top = jnp.max(scores, axis=2, keepdims=True)
+        exps = jnp.exp2((scores - top).astype(BF))
+        sums = [jnp.dot(exps[h], values[h], preferred_element_type=F32) for h in range(H)]
+        for pair in range(H // 2):
+            first, second = sums[2 * pair], sums[2 * pair + 1]
+            norm = pltpu.roll(jnp.where(low, second, first), HD, 1)
+            result = (jnp.where(low, first, second) / norm).astype(BF)
+            yield g, pair, result.reshape(sources, rows, 2 * HD)
+
+
+def block_kernel(
+    count_ref, video_hbm, video, w_space, w_os, w_time, w_ot, out,
+    x_buf, w_buf, normed, qkv, sent, spatial, ws, wt, middle, x_in, t_out, t_in,
+    loads, sem_v, sem_s, sem_a, sem_b,
+):
+    n, patches, width = x_buf.shape
+    chunks, pieces, _, _, cols = spatial.shape
+    devices, share = x_in.shape[1], x_in.shape[2]
+    z_me, t_me = lax.axis_index("space"), lax.axis_index("tm")
+    z_to = [lax.rem(z_me + d, n) for d in range(n)]
+    z_from = [lax.rem(z_me + n - d, n) for d in range(n)]
+    t_to = [lax.rem(t_me + d, devices) for d in range(devices)]
+    count = count_ref[0]
+    valid = [(t_me * n + f < count).astype(F32) for f in range(n)]
+
+    barrier = pltpu.get_barrier_semaphore()
+    for axis, peers in (("space", z_to), ("tm", t_to)):
+        for peer in peers[1:]:
+            pl.semaphore_signal(
+                barrier, inc=1, device_id={axis: peer}, device_id_type=pl.DeviceIdType.MESH
+            )
+    own = pltpu.make_async_copy(video_hbm.at[z_me], x_buf.at[z_me], loads.at[0])
+    own.start()
+    load = pltpu.make_async_copy(w_space, w_buf, loads.at[1])
+    load.start()
+    load_s = pltpu.make_async_copy(w_os, ws, loads.at[2])
+    load_t = pltpu.make_async_copy(w_ot, wt, loads.at[3])
+    pl.semaphore_wait(barrier, n + devices - 2)
+
+    def remote(src, dst, sems, i, d, axis, peer):
+        return pltpu.make_async_remote_copy(
+            src_ref=src,
+            dst_ref=dst,
+            send_sem=sems.at[0, i, d],
+            recv_sem=sems.at[1, i, d],
+            device_id={axis: peer},
+            device_id_type=pl.DeviceIdType.MESH,
+        )
+
+    def rows_in(t, d):
+        rows = pl.ds(t * STEP, STEP)
+        return remote(
+            video_hbm.at[z_to[d], rows], x_buf.at[z_me, rows], sem_v, t, d, "space", z_to[d]
+        )
+
+    def result_back(k, c, d):
+        return remote(
+            sent.at[k, c, d], spatial.at[k, c, z_me], sem_s, k * pieces + c, d, "space", z_to[d]
+        )
+
+    def forth(k, d):
+        return remote(middle.at[k, t_to[d]], x_in.at[k, t_me], sem_a, k, d, "tm", t_to[d])
+
+    def back(k, d):
+        return remote(t_out.at[k, t_to[d]], t_in.at[k, t_me], sem_b, k, d, "tm", t_to[d])
+
+    for t in range(chunks):
+        for d in range(1, n):
+            rows_in(t, d).start()
+    load_s.start()
+    load_t.start()
+    own.wait()
+    load.wait()
+
+    def project(blocks):
+        for at, (source, offset) in enumerate(blocks):
+            rows = x_buf[source, offset : offset + STEP, :]
+            normed[at * STEP : (at + 1) * STEP, :] = norm_rows(rows.astype(F32))
+
+        @pl.loop(0, 6)
+        def _(i):
+            part = pl.ds(pl.multiple_of(i * 512, 512), 512)
+            result = jnp.dot(normed[...], w_buf[:, part], preferred_element_type=F32)
+            scale = jnp.where(i < 2, 0.125 * LOG2E, 1.0).astype(F32)
+            result = (result * scale).astype(BF)
+            for at, (source, offset) in enumerate(blocks):
+                start = pl.multiple_of(source * patches + offset, STEP)
+                qkv[pl.ds(start, STEP), part] = result[at * STEP : (at + 1) * STEP]
+
+    project([(z_me, t * STEP) for t in range(chunks)])
+    for t in range(chunks):
+        for d in range(1, n):
+            rows_in(t, d).wait_recv()
+        project([(z_from[d], t * STEP) for d in range(1, n)])
+    load_q = pltpu.make_async_copy(w_time, w_buf, loads.at[4])
+    load_q.start()
+
+    low = lax.broadcasted_iota(jnp.int32, (n * STEP, 2 * HD), 1) < HD
+    low_all = lax.broadcasted_iota(jnp.int32, (n * patches, 2 * HD), 1) < HD
+
+    def attend(k):
+        @pl.loop(0, pieces)
+        def _(c):
+            keys, values, queries = [], [], []
+            for pair in range(2):
+                start = pl.multiple_of(c * cols + pair * 128, 128)
+                query = jnp.concatenate(
+                    [
+                        qkv[
+                            pl.ds(pl.multiple_of(z_to[d] * patches + k * STEP, STEP), STEP),
+                            pl.ds(start, 128),
+                        ]
+                        for d in range(n)
+                    ],
+                    axis=0,
+                )
+                zero = jnp.zeros_like(query)
+                queries.append((jnp.where(low, query, zero), jnp.where(low, zero, query)))
+                keys.append(qkv[:, pl.ds(pl.multiple_of(start + H * HD, 128), 128)])
+                value = qkv[:, pl.ds(pl.multiple_of(start + 2 * H * HD, 128), 128)]
+                one = jnp.ones_like(value)
+                values.append((jnp.where(low_all, value, one), jnp.where(low_all, one, value)))
+
+            def scores_of(pair, head):
+                return lax.dot_general(
+                    queries[pair][head],
+                    keys[pair],
+                    (((1,), (1,)), ((), ())),
+                    preferred_element_type=F32,
+                )
+
+            units = [(pair, head) for pair in range(2) for head in range(2)]
+            following = scores_of(*units[0])
+            sums = []
+            for at, (pair, head) in enumerate(units):
+                scores = following
+                if at + 1 < len(units):
+                    following = scores_of(*units[at + 1])
+                top = jnp.max(scores, axis=1, keepdims=True)
+                exps = jnp.exp2((scores - top).astype(BF))
+                sums.append(jnp.dot(exps, values[pair][head], preferred_element_type=F32))
+                if head == 1:
+                    result = jnp.where(low, sums[0], sums[1])
+                    norm = pltpu.roll(jnp.where(low, sums[1], sums[0]), HD, 1)
+                    sums = []
+                    result = (result / norm).astype(BF)
+                    place = slice(pair * 128, (pair + 1) * 128)
+                    spatial[k, c, z_me, :, place] = result[:STEP]
+                    for d in range(1, n):
+                        sent[k, c, d, :, place] = result[d * STEP : (d + 1) * STEP]
+            for d in range(1, n):
+                result_back(k, c, d).start()
+
+    def join(k):
+        @pl.loop(0, pieces)
+        def _(c):
+            for d in range(1, n):
+                result_back(k, c, d).wait_recv()
+
+        part = slice(k * STEP, (k + 1) * STEP)
+        branch = sum(
+            jnp.dot(
+                spatial[k, c].reshape(n * STEP, cols),
+                ws[c * cols : (c + 1) * cols, :],
+                preferred_element_type=F32,
+            )
+            for c in range(pieces)
+        ).reshape(n, STEP, width)
+        wide = [video[f, part, :].astype(F32) + valid[f] * branch[f] for f in range(n)]
+        middle[k] = interleave(jnp.stack(wide)).astype(BF).reshape(devices, share, width)
+        for d in range(1, devices):
+            forth(k, d).start()
+        x_in[k, t_me] = middle[k, t_me]
+
+    def over_time(k):
+        for d in range(1, devices):
+            forth(k, d).wait_recv()
+        rows = share // GROUPS
+        for g, pair, result in time_rows(x_in[k], w_buf, count):
+            t_out[k, :, g * rows : (g + 1) * rows, pair * 2 * HD : (pair + 1) * 2 * HD] = result
+        for d in range(1, devices):
+            back(k, d).start()
+        t_in[k, t_me] = t_out[k, t_me]
+
+    def finish(k):
+        for d in range(1, devices):
+            back(k, d).wait_recv()
+        branch = jnp.dot(
+            t_in[k].reshape(devices * share, H * HD), wt[...], preferred_element_type=F32
+        )
+        middles = deinterleave(middle[k].reshape(devices * share, width).astype(F32), n)
+        branches = deinterleave(branch, n)
+        for f in range(n):
+            out[f, k * STEP : (k + 1) * STEP, :] = (middles[f] + valid[f] * branches[f]).astype(BF)
+
+    attend(0)
+    attend(1)
+    load_s.wait()
+    join(0)
+    attend(2)
+    join(1)
+    load_q.wait()
+    over_time(0)
+    join(2)
+    over_time(1)
+    over_time(2)
+    load_t.wait()
+    finish(0)
+    finish(1)
+    finish(2)
+
+    for t in range(chunks):
+        for d in range(1, n):
+            rows_in(t, d).wait_send()
+            for c in range(pieces):
+                result_back(t, c, d).wait_send()
+        for d in range(1, devices):
+            forth(t, d).wait_send()
+            back(t, d).wait_send()
+
+
+def by_frame(video, frame_count, qkv_space, out_space, qkv_time, out_time):
+    n, patches, width = video.shape
+    devices = lax.axis_size("tm")
+    chunks, pieces = patches // STEP, 4
+    share = n * STEP // devices
+    tokens = n * patches
+    cols = H * HD // pieces
+    vmem = pl.BlockSpec(memory_space=pltpu.VMEM)
+    hbm = pl.BlockSpec(memory_space=pl.ANY)
+    return pl.pallas_call(
+        block_kernel,
+        in_specs=[pl.BlockSpec(memory_space=pltpu.SMEM), hbm, vmem, hbm, hbm, hbm, hbm],
+        out_specs=vmem,
+        out_shape=jax.ShapeDtypeStruct(video.shape, BF),
+        scratch_shapes=[
+            pltpu.VMEM((n, patches, width), BF),
+            pltpu.VMEM(qkv_space.shape, BF),
+            pltpu.VMEM((patches, width), BF),
+            pltpu.VMEM((tokens, 3 * H * HD), BF),
+            pltpu.VMEM((chunks, pieces, n, STEP, cols), BF),
+            pltpu.VMEM((chunks, pieces, n, STEP, cols), BF),
+            pltpu.VMEM(out_space.shape, BF),
+            pltpu.VMEM(out_time.shape, BF),
+            pltpu.VMEM((chunks, devices, share, width), BF),
+            pltpu.VMEM((chunks, devices, share, width), BF),
+            pltpu.VMEM((chunks, devices, share, H * HD), BF),
+            pltpu.VMEM((chunks, devices, share, H * HD), BF),
+            pltpu.SemaphoreType.DMA((5,)),
+            pltpu.SemaphoreType.DMA((2, chunks, n)),
+            pltpu.SemaphoreType.DMA((2, chunks * pieces, n)),
+            pltpu.SemaphoreType.DMA((2, chunks, devices)),
+            pltpu.SemaphoreType.DMA((2, chunks, devices)),
+        ],
+        compiler_params=pltpu.CompilerParams(
+            vmem_limit_bytes=VMEM_LIMIT, collective_id=0, has_side_effects=True
+        ),
+        cost_estimate=pl.CostEstimate(
+            flops=16 * tokens * width * H * HD + 4 * tokens * (tokens + 128) * H * HD,
+            bytes_accessed=2 * (3 * tokens * width + 8 * width * H * HD),
+            transcendentals=tokens * (tokens + 128) * H,
+        ),
+    )(frame_count, video, video, qkv_space, out_space, qkv_time, out_time)
+
+
+def per_device(video, *rest):
+    frames, patches, _ = video.shape
+    fits = (
+        frames == 4
+        and lax.axis_size("space") == frames
+        and lax.axis_size("tm") == 8
+        and patches == 288
+    )
+    return (by_frame if fits else general)(video, *rest)
+
+
 def solution(mesh):
     return jax.shard_map(
         per_device,

time: 668 us -> 193 us (0.29); the launches traced: 656 us -> 192 us
  blocking collectives: 246 us -> 0 us
  Pallas kernels: 0 us -> 188 us
  local copies, waits for them, and re-layouts: 136 us -> 4.02 us
  waiting for transfers between devices: 126 us -> 0 us
  matrix products: 111 us -> 0 us
  other arithmetic: 23.2 us -> 0 us
  starting transfers between devices: 13.1 us -> 0 us
    all_to_all x2 -> x0, blocking collectives: 246 us -> none  [the longest x1 209 us: per_device(): lax.all_to_all(qkv1, 'space', split_axis=3, concat_axis=1, tiled=True)]
    pallas_call x0 -> x1, Pallas kernels: none -> 188 us  [by_frame(): pl.pallas_call(block_kernel, in_specs=[pl.BlockSpec(memory_space=pltpu.SM...]
    all_to_all x2 -> x0, waiting for transfers between devices: 126 us -> none  [the longest x1 76.3 us: per_device(): lax.all_to_all(qkv2, 'tm', split_axis=1, concat_axis=0, tiled=True)]
    reshape x9 -> x0, local copies, waits for them, and re-layouts: 111 us -> none  [the longest x2 39.5 us: per_device(): qkv1 = qkv1.astype(jnp.bfloat16).reshape(frames, patches, 3, H * HD)]
    dot_general x7 -> x0, matrix products: 85.9 us -> none  [the longest x1 35 us: spatial_attend(): jnp.einsum('fhqk,fkhd->fqhd', weights, parts[:, :, 2], preferred_element_...]
    sub x1 -> x0, matrix products: 25 us -> none  [spatial_attend(): weights = jax.nn.softmax(scores, axis=-1).astype(jnp.bfloat16)]
    sub x1 -> x0, other arithmetic: 13.8 us -> none  [per_device(): weights = jax.nn.softmax(scores, axis=-1).astype(jnp.bfloat16)]
    all_to_all x3 -> x0, local copies, waits for them, and re-layouts: 13.6 us -> none  [the longest x1 9.69 us: per_device(): lax.all_to_all(qkv2, 'tm', split_axis=1, concat_axis=0, tiled=True)]
  transfers between devices with their start and end apart: 2 -> 0, of which waited for: 2 -> 0; matrix products, arithmetic and copies ran while one was open for 0% -> 0% of each run, Pallas kernels for 0% -> 0%
where the time goes in v4:
time: 193 us; the launch traced here: 192 us
  Pallas kernels  188 us (97%)
  local copies, waits for them, and re-layouts  4.02 us (2%)
    pallas_call x1, Pallas kernels, by_frame(): pl.pallas_call(block_kernel, in_specs=[pl.BlockSpec(memory_space=pltpu.SM...  188 us
    unnamed x1, local copies, waits for them, and re-layouts  4.02 us

profile of v4, /device:TPU:29, one launch (start us, length us, event | category | flops | bytes accessed | tf_op | source)
XLA Modules:
  0.0 192.2 jit_solution(2243175827806328196)
XLA Ops:
  0.7 187.5 %shard_map.64 = bf16[4,288,1536]{2,1,0:T(8,128)(2,1)} custom-call(s32[1]{0:T(128)S(6)} %copy.8.count_ref, bf16[4,288,1536]{2,1,0:T(8,128)(2,1)} %video.1, bf16[4,288,1536]{2,1,0:T(8,128)(2,1)} %video.1, bf16[1536,3072]{1,0:T(8,128)(2,1)} %w_space.1, bf16[1024,1536]{1,0:T(8,128)(2,1)} %w_os.1, bf16[1536,3072]{1,0:T(8,128)(2,1)} %w_time.1, bf16[1024,1536]{1,0:T(8,128)(2,1)} %w_ot.1), custom_call_target="tpu_custom_call" | custom-call | flops 35030827008 | bytes 35782656 | tf_op jit(solution)/shard_map/pallas_call | solution.py:386
  188.2 4.0 %copy.9 = bf16[4,288,1536]{2,1,0:T(8,128)(2,1)} copy(bf16[4,288,1536]{2,1,0:T(8,128)(2,1)} %shard_map.64) | data formatting | bytes 7077888
